TPU v7x, 32 devices: a whole 2x2x4 slice. The times are simulated.
32 devices in a mesh: gx: 4 (over y, x), gy: 2 (over core), gz: 4 (over z).
Axes of the slice: x: 2, y: 2, z: 4, core: 2. Of those that a mesh axis runs over, the one named last changes fastest.
Arguments:
- features: bfloat16 [32, 32, 64, 512], P(None, 'gx', 'gy', 'gz'), may hold values from -12 to 12
- posteriors: bfloat16 [16, 32, 64, 512], P(None, 'gx', 'gy', 'gz'), may hold values from 0 to 1, as said below
Outputs:
- segmentation: bfloat16 [16, 32, 64, 512], P(None, 'gx', 'gy', 'gz')
- class_means: float32 [16, 32], replicated
Inputs may be any that keep to these rules, and one draw needn't show every extreme that they name: Each voxel's 16 initial posteriors are positive and sum to one up to rounding.
All inputs are finite; a program needn't handle non-finite values.
Results may differ from a plain program's by a relative error of at most 0.0075.
Values may be sent and summed in bfloat16 or wider, within the bound.
No kernel may reach another device: no remote copies, remote signals or barrier semaphores. Data moves between devices by JAX's collectives and lax.ppermute only.
A program may use at most 128 MiB of HBM per device.

v0:
```python
import jax
import jax.numpy as jnp
from jax import lax
from jax.sharding import PartitionSpec as P

SWEEPS = 2


beta_coupling = 1.0
ridge = 0.1


def with_halo(x, sides, width):
    for axis, dim in sides:
        count, length = (lax.axis_size(axis), x.shape[dim])
        up = [(i, (i + 1) % count) for i in range(count - 1)]
        down = [(j, i) for i, j in up]
        last = lax.slice_in_dim(x, length - width, length, axis=dim)
        initial = lax.slice_in_dim(x, 0, width, axis=dim)
        before = lax.ppermute(last, axis, up)
        after = lax.ppermute(initial, axis, down)
        x = jnp.concatenate([before, x, after], axis=dim)
    return x


def finish(counts, total_weight, first_moment, scatter):
    identity = jnp.eye(first_moment.shape[1], dtype=jnp.float32)
    centers = first_moment / counts[:, None]
    spread = (
        scatter / counts[:, None, None]
        - centers[:, :, None] * centers[:, None, :]
        + ridge * identity
    )
    factor = jnp.linalg.cholesky(spread)
    whiten = jax.vmap(
        lambda lower_factor: jax.scipy.linalg.solve_triangular(lower_factor, identity, lower=True)
    )(factor)
    offset = jnp.einsum("kgf,kf->kg", whiten, centers, precision=lax.Precision.HIGHEST)
    biases = jnp.log(counts / total_weight) - jnp.sum(
        jnp.log(jnp.diagonal(factor, axis1=1, axis2=2)), axis=1
    )
    return (centers, whiten, offset, biases)


def local_moments(posterior, voxels):
    flat_post = posterior.reshape(posterior.shape[0], -1)
    flat_vox = voxels.reshape(voxels.shape[0], -1)
    contract = (((1,), (1,)), ((), ()))
    counts = jnp.sum(flat_post.astype(jnp.float32), axis=1)
    first_moment = lax.dot_general(
        flat_post, flat_vox, contract, preferred_element_type=jnp.float32
    )

    def second(weights_row):
        weighted = weights_row[None, :] * flat_vox
        return lax.dot_general(weighted, flat_vox, contract, preferred_element_type=jnp.float32)

    scatter = lax.map(second, flat_post)
    return (counts, first_moment, scatter)


def fit(posterior, voxels):
    counts, first_moment, scatter = local_moments(posterior, voxels)
    counts, first_moment, scatter = lax.psum((counts, first_moment, scatter), ("gx", "gy", "gz"))
    return finish(counts, jnp.sum(counts), first_moment, scatter)


def loglik(voxels, whiten, offset, biases):
    flat_vox = voxels.reshape(voxels.shape[0], -1)
    rounded = whiten.astype(jnp.bfloat16)

    def per_class(class_record):
        matrix, shift, level = class_record
        whitened = jnp.dot(matrix, flat_vox, preferred_element_type=jnp.float32) - shift[:, None]
        return level - 0.5 * jnp.sum(whitened * whitened, axis=0)

    scores = lax.map(per_class, (rounded, offset, biases))
    return scores.reshape((whiten.shape[0],) + voxels.shape[1:])


def neighbours(padded):
    inner = padded[:, 2:, 1:-1, 1:-1] + padded[:, :-2, 1:-1, 1:-1]
    inner = inner + padded[:, 1:-1, 2:, 1:-1] + padded[:, 1:-1, :-2, 1:-1]
    return inner + padded[:, 1:-1, 1:-1, 2:] + padded[:, 1:-1, 1:-1, :-2]


def state_update(scores, near_sum):
    return jax.nn.softmax(scores + beta_coupling * near_sum, axis=0).astype(jnp.bfloat16)


def local(features, posteriors):
    centers, whiten, offset, biases = fit(posteriors, features)
    scores = loglik(features, whiten, offset, biases)
    current = posteriors
    for pass_index in range(SWEEPS):
        padded = with_halo(current, (("gx", 1), ("gy", 2), ("gz", 3)), 1)
        current = state_update(scores, neighbours(padded.astype(jnp.float32)))
    centers, whiten, offset, biases = fit(current, features)
    scores = loglik(features, whiten, offset, biases)
    padded = with_halo(current, (("gx", 1), ("gy", 2), ("gz", 3)), 1)
    segmentation = state_update(scores, neighbours(padded.astype(jnp.float32)))
    return (segmentation, centers)


def solution(mesh):
    placed = (P(None, "gx", "gy", "gz"), P(None, "gx", "gy", "gz"))
    return jax.shard_map(
        local,
        mesh=mesh,
        in_specs=placed,
        out_specs=(P(None, "gx", "gy", "gz"), P()),
        check_vma=False,
    )
```

profile of v0, /device:TPU:0, one launch (start us, length us, event | category | flops | bytes accessed | tf_op | source)
XLA Modules:
  0.0 852.9 jit_solution(13357098373740108110)
XLA Ops:
  7.2 4.4 copy.131
  12.3 53.4 %while.40 = (s32[]{:T(128)}, f32[16,32,32]{1,2,0:T(8,128)S(1)}, bf16[16,32768]{1,0:T(8,128)(2,1)S(1)}, bf16[32,32768]{1,0:T(8,128)(2,1)}, s32[]{:T(128)}) while((s32[]{:T(128)}, f32[16,32,32]{1,2,0:T(8,128)S(1)}, bf16[16,32768]{1,0:T(8,128)(2,1)S(1)}, bf16[32,32768]{1,0:T(8,128)(2,1)}, s32[]{:T(128)}) %tuple.99), condition=%wide.region_1.2_spmd, body=%wide.region_0.0_spmd.sunk | while | flops 68157440 | bytes 4407873 | solution.py:58
  12.7 2.9 fusion.95
  16.1 2.9 fusion.95
  19.4 2.9 fusion.95
  22.8 2.9 fusion.95
  26.1 2.9 fusion.95
  29.4 2.9 fusion.95
  32.8 2.9 fusion.95
  36.1 2.9 fusion.95
  39.4 2.9 fusion.95
  42.8 2.9 fusion.95
  46.1 2.9 fusion.95
  49.4 2.9 fusion.95
  52.8 2.9 fusion.95
  56.1 2.9 fusion.95
  59.4 2.9 fusion.95
  62.8 2.9 fusion.95
  66.5 4.8 collective-permute-start
  72.6 3.6 fusion.38
  76.6 42.0 %all-reduce.1 = (f32[16,32]{1,0:T(8,128)S(1)}, f32[16]{0:T(128)S(1)}) all-reduce(f32[16,32]{1,0:T(8,128)S(1)} %fusion.38, f32[16]{0:T(128)S(1)} %convert_reduce_fusion.1), channel_id=1, replica_groups=mesh['gx'=4,'gy'=2,'gz'=4] {'gx','gy','gz'}, use_global_device_ids=true, to_apply=%region_5.6 | all-reduce | flops 528 | bytes 4224 | tf_op jit(solution)/shard_map/psum | solution.py:64
  119.4 74.9 %all-reduce.5.cloned.1.call-done = f32[16,32,32]{1,2,0:T(8,128)} async-done(((f32[16,32,32]{1,2,0:T(8,128)}), f32[16,32,32]{1,2,0:T(8,128)}) %all-reduce.5.cloned.1.call-update) | async-done | bytes 65552 | tf_op jit(solution)/shard_map/psum | solution.py:64
  196.7 46.9 %custom-call.12 = f32[16,32,32]{2,1,0:T(8,128)S(1)} custom-call(f32[16,32,32]{2,1,0:T(8,128)S(1)} %fusion.51), custom_call_target="Cholesky" | custom-call | tf_op jit(solution)/shard_map/jit(cholesky)/cholesky | solution.py:34
  243.9 39.4 %custom-call.13 = f32[16,1,32,32]{2,3,1,0:T(8,128)S(1)} custom-call(f32[16,1,32,32]{3,2,1,0:T(8,128)S(1)} %get-tuple-element.172), custom_call_target="InvertDiagBlocksLowerTriangular" | custom-call | tf_op jit(solution)/shard_map/vmap(jit(_solve_triangular))/triangular_solve | solution.py:36
  293.9 4.1 collective-permute-start.4
  301.4 75.4 %while.41 = (s32[]{:T(128)}, f32[16,32768]{1,0:T(8,128)S(1)}, f32[16]{0:T(128)S(1)}, bf16[16,32,32]{2,1,0:T(8,128)(2,1)S(1)}, bf16[32,32768]{1,0:T(8,128)(2,1)}, /*index=5*/f32[16,32]{1,0:T(8,128)S(1)}, s32[]{:T(128)}, s32[]{:T(128)}) while((s32[]{:T(128)}, f32[16,32768]{1,0:T(8,128)S(1)}, f32[16]{0:T(128)S(1)}, ...), condition=%wide.region_12.15_spmd, body=%wide.region_10.14_spmd.sunk | while | flops 70287360 | bytes 2761585 | solution.py:77
  380.1 3.0 copy.71
  385.9 5.0 maximum_convert_fusion
  390.9 3.2 fusion.60
  394.8 3.4 collective-permute-start.6
  401.3 4.7 collective-permute-done.7
  417.2 4.7 collective-permute-start.10
  421.9 2.9 copy.74
  426.3 2.9 copy.75
  433.8 5.6 maximum_convert_fusion.1
  439.4 3.2 fusion.58
  446.5 3.7 collective-permute-start.12
  452.2 53.2 %while.42 = (s32[]{:T(128)}, f32[16,32,32]{1,2,0:T(8,128)S(1)}, bf16[16,32768]{1,0:T(8,128)(2,1)S(1)}, bf16[32,32768]{1,0:T(8,128)(2,1)}, s32[]{:T(128)}) while((s32[]{:T(128)}, f32[16,32,32]{1,2,0:T(8,128)S(1)}, bf16[16,32768]{1,0:T(8,128)(2,1)S(1)}, bf16[32,32768]{1,0:T(8,128)(2,1)}, s32[]{:T(128)}) %tuple.101), condition=%wide.region_18.21_spmd, body=%wide.region_17.20_spmd.sunk | while | flops 68157440 | bytes 4407873 | solution.py:58
  452.6 2.9 fusion.101
  455.9 2.9 fusion.101
  459.2 2.9 fusion.101
  462.6 2.9 fusion.101
  465.9 2.9 fusion.101
  469.2 2.9 fusion.101
  472.5 2.9 fusion.101
  475.9 2.9 fusion.101
  479.2 2.9 fusion.101
  482.5 2.9 fusion.101
  485.9 2.9 fusion.101
  489.2 2.9 fusion.101
  492.5 2.9 fusion.101
  495.8 2.9 fusion.101
  499.2 2.9 fusion.101
  502.5 2.9 fusion.101
  506.1 39.6 %all-reduce = (f32[16,32]{1,0:T(8,128)S(1)}, f32[16]{0:T(128)S(1)}) all-reduce(f32[16,32]{1,0:T(8,128)S(1)} %fusion.41, f32[16]{0:T(128)S(1)} %get-tuple-element.166), channel_id=1, replica_groups=mesh['gx'=4,'gy'=2,'gz'=4] {'gx','gy','gz'}, use_global_device_ids=true, to_apply=%region_22.25 | all-reduce | flops 528 | bytes 4224 | tf_op jit(solution)/shard_map/psum | solution.py:64
  546.5 84.4 %all-reduce.7.cloned.1.call-done = f32[16,32,32]{1,2,0:T(8,128)} async-done(((f32[16,32,32]{1,2,0:T(8,128)}), f32[16,32,32]{1,2,0:T(8,128)}) %all-reduce.7.cloned.1.call-update) | async-done | bytes 65552 | tf_op jit(solution)/shard_map/psum | solution.py:64
  633.2 46.9 %custom-call.14 = f32[16,32,32]{2,1,0:T(8,128)S(1)} custom-call(f32[16,32,32]{2,1,0:T(8,128)S(1)} %fusion.48), custom_call_target="Cholesky" | custom-call | tf_op jit(solution)/shard_map/jit(cholesky)/cholesky | solution.py:34
  680.4 39.4 %custom-call.15 = f32[16,1,32,32]{2,3,1,0:T(8,128)S(1)} custom-call(f32[16,1,32,32]{3,2,1,0:T(8,128)S(1)} %get-tuple-element.164), custom_call_target="InvertDiagBlocksLowerTriangular" | custom-call | tf_op jit(solution)/shard_map/vmap(jit(_solve_triangular))/triangular_solve | solution.py:36
  731.3 2.9 copy.84
  734.2 3.9 collective-permute-start.16
  741.8 86.8 %while.43 = (s32[]{:T(128)}, f32[16,32768]{1,0:T(8,128)S(1)}, f32[16]{0:T(128)S(1)}, bf16[16,32,32]{2,1,0:T(8,128)(2,1)}, bf16[32,32768]{1,0:T(8,128)(2,1)}, /*index=5*/f32[16,32]{1,0:T(8,128)}, s32[]{:T(128)}, s32[]{:T(128)}) while((s32[]{:T(128)}, f32[16,32768]{1,0:T(8,128)S(1)}, f32[16]{0:T(128)S(1)}, bf16[16,32,32]{2,1,0:T(8,128)(2,1)}, ...), condition=%wide.region_27.30_spmd, body=%wide.region_25.29_spmd.sunk | while | flops 70287360 | bytes 2761709 | solution.py:77
  832.4 2.9 copy.87
  835.3 5.4 maximum_convert_fusion.2
  840.8 3.1 fusion.56
  (341 shorter events, 252.1 us)
Async XLA Ops:
  7.2 187.2 %all-reduce.5.cloned.1.call-start = ((), (), s32[]{:S(2)}) async-start(), calls=%async_computation | async-start | bytes 524288 | tf_op jit(solution)/shard_map/psum | solution.py:64
  7.2 4.4 copy-start
  65.7 0.7 copy-start.6
  66.4 564.4 %all-reduce.7.cloned.1.call-start = ((), (), s32[]{:S(2)}) async-start(), calls=%async_computation.1 | async-start | bytes 524288 | tf_op jit(solution)/shard_map/psum | solution.py:64
  66.5 218.9 %collective-permute-start = (bf16[16,1,32,128]{3,2,1,0:T(8,128)(2,1)S(1)}, bf16[16,1,32,128]{3,2,1,0:T(8,128)(2,1)S(1)}, u32[]{:S(2)}, u32[]{:S(2)}) collective-permute-start(bf16[16,1,32,128]{3,2,1,0:T(8,128)(2,1)S(1)} %get-tuple-element.191), channel_id=1, source_target_pairs={{0,8},{8,16},{16,24},{1,9},{9,17},{17,25},{2,10},{10,18},{18,26},{... | collective-permute-start | bytes 393224 | tf_op jit(solution)/shard_map/ppermute | solution.py:20
  71.3 214.3 %collective-permute-start.1 = (bf16[16,1,32,128]{3,2,1,0:T(8,128)(2,1)S(1)}, bf16[16,1,32,128]{3,2,1,0:T(8,128)(2,1)S(1)}, u32[]{:S(2)}, u32[]{:S(2)}) collective-permute-start(bf16[16,1,32,128]{3,2,1,0:T(8,128)(2,1)S(1)} %get-tuple-element.190), channel_id=1, source_target_pairs={{8,0},{16,8},{24,16},{9,1},{17,9},{25,17},{10,2},{18,10},{26,18},{... | collective-permute-start | bytes 393224 | tf_op jit(solution)/shard_map/ppermute | solution.py:21
  76.5 207.9 %copy-start.8 = (f32[32,32]{0,1:T(8,128)}, f32[32,32]{0,1:T(8,128)S(1)}, u32[]{:S(2)}) copy-start(f32[32,32]{0,1:T(8,128)S(1)} %fusion.55) | copy-start | bytes 12292
  76.6 208.1 %copy-start.19 = (pred[32,32]{1,0:T(8,128)(4,1)}, pred[32,32]{1,0:T(8,128)(4,1)S(1)}, u32[]{:S(2)}) copy-start(pred[32,32]{1,0:T(8,128)(4,1)S(1)} %iota_compare_fusion) | copy-start | bytes 3076
  119.4 165.2 %copy-start.17 = (f32[32,32]{1,0:T(8,128)}, f32[32,32]{1,0:T(8,128)S(1)}, u32[]{:S(2)}) copy-start(f32[32,32]{1,0:T(8,128)S(1)} %copy.67) | copy-start | bytes 12292
  285.7 4.6 copy-start.3
  285.8 3.8 collective-permute-start.2
  287.1 3.2 collective-permute-start.3
  290.3 0.6 copy-start.14
  293.9 7.4 copy-start.21
  293.9 86.1 %collective-permute-start.4 = (bf16[16,10,34,1]{2,0,3,1:T(8,128)(2,1)S(1)}, bf16[16,10,34,1]{2,0,3,1:T(8,128)(2,1)}, u32[]{:S(2)}, u32[]{:S(2)}) collective-permute-start(bf16[16,10,34,1]{2,0,3,1:T(8,128)(2,1)S(1)} %copy.69), channel_id=1, source_target_pairs={{0,1},{1,2},{2,3},{4,5},{5,6},{6,7},{8,9},{9,10},{10,11},{12,13},{... | collective-permute-start | bytes 32648 | tf_op jit(solution)/shard_map/ppermute | solution.py:20
  299.9 83.1 %collective-permute-start.5 = (bf16[16,10,34,1]{2,0,3,1:T(8,128)(2,1)}, bf16[16,10,34,1]{2,0,3,1:T(8,128)(2,1)}, u32[]{:S(2)}, u32[]{:S(2)}) collective-permute-start(bf16[16,10,34,1]{2,0,3,1:T(8,128)(2,1)} %copy.70), channel_id=1, source_target_pairs={{1,0},{2,1},{3,2},{5,4},{6,5},{7,6},{9,8},{10,9},{11,10},{13,12},{... | collective-permute-start | bytes 32648 | tf_op jit(solution)/shard_map/ppermute | solution.py:21
  376.8 1.3 copy-start.1
  380.1 5.8 copy-start.4
  394.8 6.5 collective-permute-start.6
  398.2 7.9 collective-permute-start.7
  406.1 2.8 collective-permute-start.8
  407.6 3.2 collective-permute-start.9
  410.8 0.6 copy-start.15
  417.2 9.1 %collective-permute-start.10 = (bf16[16,10,34,1]{2,0,3,1:T(8,128)(2,1)S(1)}, bf16[16,10,34,1]{2,0,3,1:T(8,128)(2,1)}, u32[]{:S(2)}, u32[]{:S(2)}) collective-permute-start(bf16[16,10,34,1]{2,0,3,1:T(8,128)(2,1)S(1)} %copy.73), channel_id=1, source_target_pairs={{0,1},{1,2},{2,3},{4,5},{5,6},{6,7},{8,9},{9,10},{10,11},{12,13},{... | collective-permute-start | bytes 32648 | tf_op jit(solution)/shard_map/ppermute | solution.py:20
  424.8 6.2 collective-permute-start.11
  442.9 1.6 copy-start.5
  446.5 276.7 %collective-permute-start.12 = (bf16[16,1,32,128]{3,2,1,0:T(8,128)(2,1)S(1)}, bf16[16,1,32,128]{3,2,1,0:T(8,128)(2,1)S(1)}, u32[]{:S(2)}, u32[]{:S(2)}) collective-permute-start(bf16[16,1,32,128]{3,2,1,0:T(8,128)(2,1)S(1)} %get-tuple-element.186), channel_id=1, source_target_pairs={{0,8},{8,16},{16,24},{1,9},{9,17},{17,25},{2,10},{10,18},{18,26},{... | collective-permute-start | bytes 393224 | tf_op jit(solution)/shard_map/ppermute | solution.py:20
  450.2 273.1 %collective-permute-start.13 = (bf16[16,1,32,128]{3,2,1,0:T(8,128)(2,1)S(1)}, bf16[16,1,32,128]{3,2,1,0:T(8,128)(2,1)S(1)}, u32[]{:S(2)}, u32[]{:S(2)}) collective-permute-start(bf16[16,1,32,128]{3,2,1,0:T(8,128)(2,1)S(1)} %get-tuple-element.187), channel_id=1, source_target_pairs={{8,0},{16,8},{24,16},{9,1},{17,9},{25,17},{10,2},{18,10},{26,18},{... | collective-permute-start | bytes 393224 | tf_op jit(solution)/shard_map/ppermute | solution.py:21
  452.2 178.7 %copy-start.9 = (f32[32,32]{0,1:T(8,128)S(1)}, f32[32,32]{0,1:T(8,128)}, u32[]{:S(2)}) copy-start(f32[32,32]{0,1:T(8,128)} %copy-done.8) | copy-start | bytes 12292
  505.4 0.7 copy-start.7
  505.4 174.7 %copy-start.20 = (pred[32,32]{1,0:T(8,128)(4,1)S(1)}, pred[32,32]{1,0:T(8,128)(4,1)}, u32[]{:S(2)}) copy-start(pred[32,32]{1,0:T(8,128)(4,1)} %copy-done.19) | copy-start | bytes 3076
  505.4 214.4 %copy-start.18 = (f32[32,32]{1,0:T(8,128)S(1)}, f32[32,32]{1,0:T(8,128)}, u32[]{:S(2)}) copy-start(f32[32,32]{1,0:T(8,128)} %copy-done.17) | copy-start | bytes 12292
  545.8 176.6 %copy-start.16 = (f32[16,32]{1,0:T(8,128)}, f32[16,32]{1,0:T(8,128)S(1)}, u32[]{:S(2)}) copy-start(f32[16,32]{1,0:T(8,128)S(1)} %broadcast_divide_fusion) | copy-start | bytes 6148
  723.4 3.3 collective-permute-start.14
  724.7 3.2 collective-permute-start.15
  726.6 1.2 copy-start.10
  727.8 0.6 copy-start.12
  734.2 96.1 %collective-permute-start.16 = (bf16[16,10,34,1]{2,0,3,1:T(8,128)(2,1)}, bf16[16,10,34,1]{2,0,3,1:T(8,128)(2,1)}, u32[]{:S(2)}, u32[]{:S(2)}) collective-permute-start(bf16[16,10,34,1]{2,0,3,1:T(8,128)(2,1)} %copy.84), channel_id=1, source_target_pairs={{0,1},{1,2},{2,3},{4,5},{5,6},{6,7},{8,9},{9,10},{10,11},{12,13},{... | collective-permute-start | bytes 32648 | tf_op jit(solution)/shard_map/ppermute | solution.py:20
  740.1 92.4 %collective-permute-start.17 = (bf16[16,10,34,1]{2,0,3,1:T(8,128)(2,1)}, bf16[16,10,34,1]{2,0,3,1:T(8,128)(2,1)}, u32[]{:S(2)}, u32[]{:S(2)}) collective-permute-start(bf16[16,10,34,1]{2,0,3,1:T(8,128)(2,1)} %copy.85), channel_id=1, source_target_pairs={{1,0},{2,1},{3,2},{5,4},{6,5},{7,6},{9,8},{10,9},{11,10},{13,12},{... | collective-permute-start | bytes 32648 | tf_op jit(solution)/shard_map/ppermute | solution.py:21
  830.4 4.9 copy-start.11
  830.4 4.9 copy-start.13
  835.3 5.5 copy-start.2
Sparse Core Ops, SparseCore 0:
  66.6 127.7 all-reduce.4
  506.3 124.5 all-reduce.6
where the time goes:
time: 864 us; the launch traced here: 853 us
  other arithmetic  233 us (27%)
  matrix products  182 us (21%)
  waiting for transfers between devices  171 us (20%)
  local copies, waits for them, and re-layouts  127 us (15%)
  blocking collectives  81.6 us (9%)
  starting transfers between devices  40.8 us (5%)
  between operations  15.2 us (2%)
    psum x2, waiting for transfers between devices, fit(): lax.psum((counts, first_moment, scatter), ('gx', 'gy', 'gz'))  159 us
    another operation x7, other arithmetic, finish(): factor = jnp.linalg.cholesky(spread)  94.1 us
    dot_general x32, matrix products, second(): lax.dot_general(weighted, flat_vox, contract, preferred_element_type=jnp....  93.2 us
    psum x2, blocking collectives, fit(): lax.psum((counts, first_moment, scatter), ('gx', 'gy', 'gz'))  81.6 us
    dot_general x32, matrix products, per_class(): jnp.dot(matrix, flat_vox, preferred_element_type=jnp.float32)  79.2 us
    another operation x4, other arithmetic, finish(): jax.scipy.linalg.solve_triangular(lower_factor, identity, lower=True)  79 us
    dynamic_update_slice x32, local copies, waits for them, and re-layouts, loglik(): scores = lax.map(per_class, (rounded, offset, biases))  30.3 us
    ppermute x9, starting transfers between devices, with_halo(): before = lax.ppermute(last, axis, up)  28.6 us
  transfers between devices with their start and end apart: 20, of which 8 were waited for; matrix products, arithmetic and copies ran while one was open for 50% of the time, Pallas kernels for 0%

commit v1 on v0

v1 whole, which is shorter than its diff:
```python
import functools

import jax
import jax.numpy as jnp
from jax import lax
from jax.experimental import pallas as pl
from jax.experimental.pallas import tpu as pltpu
from jax.sharding import PartitionSpec as P

BETA = 1.0
RIDGE = 0.1
AXES = ("gx", "gy", "gz")
ROWS_ROWS = (((1,), (1,)), ((), ()))
VMEM_BYTES = 60 * 2**20
f32, bf16 = jnp.float32, jnp.bfloat16


def lane_iota(shape):
    return lax.broadcasted_iota(jnp.int32, shape, len(shape) - 1)


def moments_of(x, q):
    ny = x.shape[0]
    xs = jnp.concatenate([x[y] for y in range(ny)], axis=1)
    qs = jnp.concatenate([q[y] for y in range(ny)], axis=1)
    weighted = jnp.concatenate([xs[f : f + 1] * qs for f in range(xs.shape[0])], axis=0)
    ones = jnp.ones((16, xs.shape[1]), bf16)
    scatter = lax.dot_general(xs, weighted, ROWS_ROWS, preferred_element_type=f32)
    first = lax.dot_general(
        qs, jnp.concatenate([xs, ones], axis=0), ROWS_ROWS, preferred_element_type=f32
    )
    return scatter, first


def add_moments(out_ref, x, q, start):
    scatter, first = moments_of(x, q)
    feats, lanes = scatter.shape
    pieces = [scatter[:, j : j + 128] for j in range(0, lanes, 128)]
    first = jnp.pad(first, ((0, 0), (0, 128 - first.shape[1])))
    all_of = jnp.concatenate(pieces + [first], axis=0)

    @pl.when(start)
    def _():
        out_ref[...] = all_of

    @pl.when(jnp.logical_not(start))
    def _():
        out_ref[...] += all_of


def m_step(total_ref, w_ref, bias_ref):
    classes = bias_ref.shape[0]
    feats = w_ref.shape[0] // classes
    per = 128 // classes
    first = total_ref[pl.ds(total_ref.shape[0] - classes, classes), :]
    lane = lane_iota((classes, 128))
    counts = jnp.broadcast_to(first[:, feats : feats + 1], (classes, 128))
    inv = 1.0 / counts
    means = first / counts
    shifted = pltpu.roll(means, feats, 1)
    inside = (lane >= feats) & (lane < 2 * feats)
    rows = []
    for t in range(feats // per):
        block = total_ref[pl.ds(t * feats, feats), :]
        wide = jnp.concatenate(
            [jnp.zeros((feats, 128), f32), block, jnp.zeros((128 - 2 * feats, 128), f32)], axis=0
        )
        turned = wide.T
        for s in range(per):
            f = t * per + s
            mean_f = jnp.broadcast_to(means[:, f : f + 1], (classes, 128))
            spread = turned[s * classes : (s + 1) * classes] * inv - mean_f * shifted
            spread = spread + jnp.where(lane == feats + f, RIDGE, 0.0)
            rest = jnp.where(lane == 2 * feats, mean_f, jnp.where(lane == f, 1.0, 0.0))
            rows.append(jnp.where(inside, spread, rest))
    logdet = jnp.zeros((classes, 128), f32)
    for p in range(feats):
        row = rows[p]
        pivot = jnp.broadcast_to(row[:, feats + p : feats + p + 1], (classes, 128))
        scaled = row * (1.0 / pivot)
        for i in range(p + 1, feats):
            factor = jnp.broadcast_to(row[:, feats + i : feats + i + 1], (classes, 128))
            rows[i] = rows[i] - factor * scaled
        logdet = logdet + jnp.log(pivot)
        white = row * lax.rsqrt(pivot)
        shift = -jnp.broadcast_to(white[:, 2 * feats : 2 * feats + 1], (classes, 128))
        high = shift.astype(bf16).astype(f32)
        middle = (shift - high).astype(bf16).astype(f32)
        low = shift - high - middle
        parts = jnp.where(
            lane == feats, high, jnp.where(lane == feats + 1, middle, jnp.where(lane == feats + 2, low, 0.0))
        )
        white = jnp.where(lane < feats, white, parts)
        w_ref[pl.ds(p * classes, classes), :] = white[:, : feats + 16].astype(bf16)
    total = jnp.sum(counts, axis=0, keepdims=True)
    bias_ref[...] = jnp.log(counts / total) - 0.5 * logdet
    return means


def loglik_of(x, w_ref, bias):
    n, feats, nz = x.shape
    classes = bias.shape[0]
    xs = jnp.concatenate([x[j] for j in range(n)], axis=1)
    xs = jnp.concatenate([xs, jnp.ones((16, n * nz), bf16)], axis=0)
    white = jnp.dot(w_ref[...], xs, preferred_element_type=f32)
    white = white * white
    square = white[:classes]
    for g in range(1, feats):
        square = square + white[g * classes : (g + 1) * classes]
    return jnp.stack(
        [bias[:, :nz] - 0.5 * square[:, j * nz : (j + 1) * nz] for j in range(n)], axis=0
    )


def shift_matrix(ny, nz):
    src = lax.broadcasted_iota(jnp.int32, (nz + 128, nz), 0)
    dst = lax.broadcasted_iota(jnp.int32, (nz + 128, nz), 1)
    near = (src < nz) & ((src == dst + 1) | (src == dst - 1))
    face = src - nz
    high = (face >= 0) & (face < ny) & (dst == nz - 1)
    low = (face >= ny) & (face < 2 * ny) & (dst == 0)
    return jnp.where(near | high | low, 1.0, 0.0).astype(bf16)


def take_matrix(ny, nz):
    src = lax.broadcasted_iota(jnp.int32, (nz, 128), 0)
    dst = lax.broadcasted_iota(jnp.int32, (nz, 128), 1)
    hit = ((src == 0) & (dst < ny)) | ((src == nz - 1) & (dst >= ny) & (dst < 2 * ny))
    return jnp.where(hit, 1.0, 0.0).astype(bf16)


def own_lane(ny, classes):
    lane = lane_iota((ny, classes, 128))
    y = lax.broadcasted_iota(jnp.int32, (ny, classes, 128), 0)
    return (lane == y) | (lane == ny + y)


def near_of(i, nx, q_ref, x_before, x_after, y_before, y_after, z_before, z_after, flags):
    ny, classes, nz = q_ref.shape[1:]
    mid = q_ref[i]
    down = jnp.where(i > 0, q_ref[jnp.maximum(i - 1, 0)], x_before[...]).astype(f32)
    up = jnp.where(i < nx - 1, q_ref[jnp.minimum(i + 1, nx - 1)], x_after[...]).astype(f32)
    mid32 = mid.astype(f32)
    first = y_before[pl.ds(i, 1)].astype(f32) * flags[0]
    last = y_after[pl.ds(i, 1)].astype(f32) * flags[1]
    left = jnp.concatenate([first, mid32[:-1]], axis=0)
    right = jnp.concatenate([mid32[1:], last], axis=0)
    lane = lane_iota((classes, 128))
    face = jnp.where(lane < ny, z_after[i].astype(f32), z_before[i].astype(f32))
    face = jnp.where(own_lane(ny, classes), face[None], 0.0).astype(bf16)
    both = jnp.concatenate([mid, face], axis=2).reshape(ny * classes, nz + 128)
    along = jnp.dot(both, shift_matrix(ny, nz), preferred_element_type=f32)
    return (down + up) + (left + right) + along.reshape(ny, classes, nz)


def update_of(scores, near):
    s = scores + BETA * near
    e = jnp.exp(s - jnp.max(s, axis=1, keepdims=True))
    return (e * (1.0 / jnp.sum(e, axis=1, keepdims=True))).astype(bf16)


def put_faces(i, nx, q, xlo, xhi, yface, zface):
    ny, classes, nz = q.shape

    @pl.when(i == 0)
    def _():
        xlo[...] = q

    @pl.when(i == nx - 1)
    def _():
        xhi[...] = q

    yface[0, pl.ds(i, 1)] = q[0:1]
    yface[1, pl.ds(i, 1)] = q[ny - 1 : ny]
    spread = jnp.dot(q.reshape(ny * classes, nz), take_matrix(ny, nz), preferred_element_type=f32)
    spread = jnp.where(own_lane(ny, classes), spread.reshape(ny, classes, 128), 0.0)
    zface[pl.ds(i, 1)] = jnp.sum(spread, axis=0, keepdims=True).astype(bf16)


def first_kernel(x_ref, q_ref, xt, qt, xlo, xhi, yface, zface, mom):
    nx = x_ref.shape[1]

    def slab(i, carry):
        x = jnp.swapaxes(x_ref[:, i], 0, 1)
        q = jnp.swapaxes(q_ref[:, i], 0, 1)
        xt[i] = x
        qt[i] = q
        put_faces(i, nx, q, xlo, xhi, yface, zface)
        add_moments(mom, x, q, i == 0)
        return carry

    lax.fori_loop(0, nx, slab, 0)


def second_kernel(flags_ref, total, xt, qt, xb, xa, yb, ya, zb, za, sc, q1, xlo, xhi, yface, zface, w, bias):
    nx = xt.shape[0]
    m_step(total, w, bias)
    flags = (flags_ref[0], flags_ref[1])

    def slab(i, carry):
        half = xt.shape[1] // 2
        sc[i, pl.ds(0, half)] = loglik_of(xt[i, pl.ds(0, half)], w, bias[...])
        sc[i, pl.ds(half, half)] = loglik_of(xt[i, pl.ds(half, half)], w, bias[...])
        q = update_of(sc[i], near_of(i, nx, qt, xb, xa, yb, ya, zb, za, flags))
        q1[i] = q
        put_faces(i, nx, q, xlo, xhi, yface, zface)
        return carry

    lax.fori_loop(0, nx, slab, 0)


def third_kernel(flags_ref, sc, xt, qt, xb, xa, yb, ya, zb, za, q2, xlo, xhi, yface, zface, mom):
    nx = xt.shape[0]
    flags = (flags_ref[0], flags_ref[1])

    def slab(i, carry):
        q = update_of(sc[i], near_of(i, nx, qt, xb, xa, yb, ya, zb, za, flags))
        q2[i] = q
        put_faces(i, nx, q, xlo, xhi, yface, zface)
        add_moments(mom, xt[i], q, i == 0)
        return carry

    lax.fori_loop(0, nx, slab, 0)


def fourth_kernel(flags_ref, total, xt, qt, xb, xa, yb, ya, zb, za, seg, means_ref, w, bias):
    nx = xt.shape[0]
    means = m_step(total, w, bias)
    means_ref[...] = means[:, : means_ref.shape[1]]
    flags = (flags_ref[0], flags_ref[1])

    def slab(i, carry):
        half = xt.shape[1] // 2
        scores = jnp.concatenate(
            [loglik_of(xt[i, pl.ds(j * half, half)], w, bias[...]) for j in range(2)], axis=0
        )
        q = update_of(scores, near_of(i, nx, qt, xb, xa, yb, ya, zb, za, flags))
        seg[:, i] = jnp.swapaxes(q, 0, 1)
        return carry

    lax.fori_loop(0, nx, slab, 0)


def sum_over_devices(x):
    for axis in ("gy", "gx", "gz"):
        n = lax.axis_size(axis)
        step = 1
        if n & (n - 1):
            x = lax.psum(x, axis)
            continue
        while step < n:
            x = x + lax.ppermute(x, axis, [(i, i ^ step) for i in range(n)])
            step *= 2
    return x


def exchange(xlo, xhi, yface, zface):
    def shift(value, axis, up):
        n = lax.axis_size(axis)
        pairs = [(i, i + 1) for i in range(n - 1)]
        return lax.ppermute(value, axis, pairs if up else [(j, i) for i, j in pairs])

    xb, xa = shift(xhi, "gx", True), shift(xlo, "gx", False)
    if lax.axis_size("gy") == 2:
        other = lax.ppermute(yface, "gy", [(0, 1), (1, 0)])
        yb, ya = other[1], other[0]
    else:
        yb, ya = shift(yface[1], "gy", True), shift(yface[0], "gy", False)
    zb, za = shift(zface, "gz", True), shift(zface, "gz", False)
    return xb, xa, yb, ya, zb, za


def call(kernel, outs, scratch, smem, *args):
    vmem = pl.BlockSpec(memory_space=pltpu.VMEM)
    specs = [pl.BlockSpec(memory_space=pltpu.SMEM)] * smem + [vmem] * (len(args) - smem)
    return pl.pallas_call(
        kernel,
        out_shape=tuple(outs),
        in_specs=specs,
        out_specs=tuple(vmem for _ in outs),
        scratch_shapes=scratch,
        compiler_params=pltpu.CompilerParams(vmem_limit_bytes=VMEM_BYTES),
    )(*args)


def local(features, posteriors):
    feats, nx, ny, nz = features.shape
    classes = posteriors.shape[0]
    shape = jax.ShapeDtypeStruct
    brick = shape((nx, ny, classes, nz), bf16)
    faces = [
        shape((ny, classes, nz), bf16),
        shape((ny, classes, nz), bf16),
        shape((2, nx, classes, nz), bf16),
        shape((nx, classes, 128), bf16),
    ]
    mom = shape((feats * feats * classes // 128 + classes, 128), f32)
    solved = [pltpu.VMEM((feats * classes, feats + 16), bf16), pltpu.VMEM((classes, 128), f32)]
    at, n = lax.axis_index("gy"), lax.axis_size("gy")
    flags = jnp.stack([at > 0, at < n - 1]).astype(f32)

    xt, qt, *edge, part = call(
        first_kernel, [shape((nx, ny, feats, nz), bf16), brick, *faces, mom], [], 0, features, posteriors
    )
    total = sum_over_devices(part)
    halo = exchange(*edge)
    sc, q1, *edge = call(
        second_kernel, [shape((nx, ny, classes, nz), f32), brick, *faces], solved, 1, flags, total, xt, qt, *halo
    )
    halo = exchange(*edge)
    q2, *edge, part = call(third_kernel, [brick, *faces, mom], [], 1, flags, sc, xt, q1, *halo)
    total = sum_over_devices(part)
    halo = exchange(*edge)
    return call(
        fourth_kernel,
        [shape(posteriors.shape, bf16), shape((classes, feats), f32)],
        solved,
        1,
        flags,
        total,
        xt,
        q2,
        *halo,
    )


def solution(mesh):
    placed = P(None, "gx", "gy", "gz")
    return jax.shard_map(
        local, mesh=mesh, in_specs=(placed, placed), out_specs=(placed, P()), check_vma=False
    )
```

time: 864 us -> 152 us (0.18); the launches traced: 853 us -> 152 us
  other arithmetic: 233 us -> 3.72 us
  matrix products: 182 us -> 0 us
  waiting for transfers between devices: 171 us -> 26.6 us
  local copies, waits for them, and re-layouts: 127 us -> 3.89 us
  blocking collectives: 81.6 us -> 0 us
  Pallas kernels: 0 us -> 69.5 us
  between operations: 15.2 us -> 0.95 us
    dot_general x68 -> x0, matrix products: 180 us -> none  [the longest x32 93.2 us: second(): lax.dot_general(weighted, flat_vox, contract, preferred_element_type=jnp....]
    another operation x11 -> x0, other arithmetic: 173 us -> none  [the longest x7 94.1 us: finish(): factor = jnp.linalg.cholesky(spread)]
    psum x2 -> x0, waiting for transfers between devices: 159 us -> none  [fit(): lax.psum((counts, first_moment, scatter), ('gx', 'gy', 'gz'))]
    psum x2 -> x0, blocking collectives: 81.6 us -> none  [fit(): lax.psum((counts, first_moment, scatter), ('gx', 'gy', 'gz'))]
    pallas_call x0 -> x4, Pallas kernels: none -> 69.5 us  [call(): pl.pallas_call(kernel, out_shape=tuple(outs), in_specs=specs, out_specs=t...]
    dynamic_slice x64 -> x0, local copies, waits for them, and re-layouts: 33.4 us -> none  [the longest x32 20.2 us: loglik(): scores = lax.map(per_class, (rounded, offset, biases))]
    dynamic_update_slice x32 -> x0, local copies, waits for them, and re-layouts: 30.3 us -> none  [loglik(): scores = lax.map(per_class, (rounded, offset, biases))]
    sub x34 -> x0, other arithmetic: 21.8 us -> none  [the longest x32 19.9 us: per_class(): return level - 0.5 * jnp.sum(whitened * whitened, axis=0)]
  transfers between devices with their start and end apart: 20 -> 25, of which waited for: 8 -> 10; matrix products, arithmetic and copies ran while one was open for 50% -> 2% of each run, Pallas kernels for 0% -> 0%
where the time goes in v1:
time: 152 us
  Pallas kernels  69.5 us (46%)
  starting transfers between devices  47.2 us (31%)
  waiting for transfers between devices  26.6 us (18%)
  local copies, waits for them, and re-layouts  3.89 us (3%)
  other arithmetic  3.72 us (2%)
    pallas_call x4, Pallas kernels, call(): pl.pallas_call(kernel, out_shape=tuple(outs), in_specs=specs, out_specs=t...  69.5 us
    ppermute x12, starting transfers between devices, shift(): lax.ppermute(value, axis, pairs if up else [(j, i) for i, j in pairs])  32.8 us
    ppermute x10, waiting for transfers between devices, sum_over_devices(): x = x + lax.ppermute(x, axis, [(i, i ^ step) for i in range(n)])  20.9 us
    ppermute x10, starting transfers between devices, sum_over_devices(): x = x + lax.ppermute(x, axis, [(i, i ^ step) for i in range(n)])  14.3 us
    ppermute x12, waiting for transfers between devices, shift(): lax.ppermute(value, axis, pairs if up else [(j, i) for i, j in pairs])  5.67 us
    add x10, other arithmetic, sum_over_devices(): x = x + lax.ppermute(x, axis, [(i, i ^ step) for i in range(n)])  3.14 us
  transfers between devices with their start and end apart: 25, of which 10 were waited for; matrix products, arithmetic and copies ran while one was open for 2% of the time, Pallas kernels for 0%

profile of v1, /device:TPU:0, one launch (start us, length us, event | category | flops | bytes accessed | tf_op | source)
XLA Modules:
  0.0 151.9 jit_solution(15427382541943239432)
XLA Ops:
  0.6 15.5 %shard_map.41 = (bf16[8,32,32,128]{3,2,1,0:T(8,128)(2,1)}, bf16[8,32,16,128]{3,2,1,0:T(8,128)(2,1)}, bf16[32,16,128]{2,1,0:T(8,128)(2,1)}, bf16[32,16,128]{2,1,0...) custom-call(bf16[32,8,32,128]{3,2,1,0:T(8,128)(2,1)} %x_ref.1, ...), custom_call_target="tpu_custom_call" | custom-call | tf_op jit(solution)/shard_map/pallas_call | solution.py:276
  16.1 0.5 collective-permute-start
  16.6 1.1 collective-permute-done
  17.7 0.9 add.30
  18.6 2.9 %collective-permute-start.1 = (f32[144,128]{1,0:T(8,128)S(1)}, f32[144,128]{1,0:T(8,128)S(1)}, u32[]{:S(2)}, u32[]{:S(2)}) collective-permute-start(f32[144,128]{1,0:T(8,128)S(1)} %add.30), channel_id=1, source_target_pairs={{0,8},{8,0},{16,24},{24,16},{1,9},{9,1},{17,25},{25,17},{2,10},{10... | collective-permute-start | bytes 221192 | tf_op jit(solution)/shard_map/ppermute | solution.py:252
  21.5 2.6 %collective-permute-done.1 = f32[144,128]{1,0:T(8,128)S(1)} collective-permute-done((f32[144,128]{1,0:T(8,128)S(1)}, f32[144,128]{1,0:T(8,128)S(1)}, u32[]{:S(2)}, u32[]{:S(2)}) %collective-permute-start.1) | collective-permute-done | bytes 73760 | tf_op jit(solution)/shard_map/ppermute | solution.py:252
  24.1 1.9 %collective-permute-start.2 = (f32[144,128]{1,0:T(8,128)S(1)}, f32[144,128]{1,0:T(8,128)S(1)}, u32[]{:S(2)}, u32[]{:S(2)}) collective-permute-start(f32[144,128]{1,0:T(8,128)S(1)} %add.31), channel_id=1, source_target_pairs={{0,16},{8,24},{16,0},{24,8},{1,17},{9,25},{17,1},{25,9},{2,18},{10... | collective-permute-start | bytes 221192 | tf_op jit(solution)/shard_map/ppermute | solution.py:252
  25.9 1.3 collective-permute-start.9
  27.2 4.5 %collective-permute-start.8 = (bf16[8,16,128]{2,1,0:T(8,128)(2,1)}, bf16[8,16,128]{2,1,0:T(8,128)(2,1)S(1)}, u32[]{:S(2)}, u32[]{:S(2)}) collective-permute-start(bf16[8,16,128]{2,1,0:T(8,128)(2,1)} %get-tuple-element.27), channel_id=1, source_target_pairs={{0,1},{1,2},{2,3},{4,5},{5,6},{6,7},{8,9},{9,10},{10,11},{12,13},{... | collective-permute-start | bytes 98312 | tf_op jit(solution)/shard_map/ppermute | solution.py:261
  31.8 0.1 collective-permute-start.7
  31.9 3.4 %collective-permute-start.5 = (bf16[32,16,128]{2,1,0:T(8,128)(2,1)}, bf16[32,16,128]{2,1,0:T(8,128)(2,1)S(1)}, u32[]{:S(2)}, u32[]{:S(2)}) collective-permute-start(bf16[32,16,128]{2,1,0:T(8,128)(2,1)} %get-tuple-element.24), channel_id=1, source_target_pairs={{0,8},{8,16},{16,24},{1,9},{9,17},{17,25},{2,10},{10,18},{18,26},{... | collective-permute-start | bytes 393224 | tf_op jit(solution)/shard_map/ppermute | solution.py:261
  35.3 0.0 collective-permute-done.2
  35.3 1.6 %collective-permute-start.3 = (f32[144,128]{1,0:T(8,128)S(1)}, f32[144,128]{1,0:T(8,128)S(1)}, u32[]{:S(2)}, u32[]{:S(2)}) collective-permute-start(f32[144,128]{1,0:T(8,128)S(1)} %add.32), channel_id=1, source_target_pairs={{0,1},{1,0},{2,3},{3,2},{4,5},{5,4},{6,7},{7,6},{8,9},{9,8},{10,11... | collective-permute-start | bytes 221192 | tf_op jit(solution)/shard_map/ppermute | solution.py:252
  37.0 0.6 add_convert_fusion.flags_ref
  37.5 2.2 %collective-permute-done.3 = f32[144,128]{1,0:T(8,128)S(1)} collective-permute-done((f32[144,128]{1,0:T(8,128)S(1)}, f32[144,128]{1,0:T(8,128)S(1)}, u32[]{:S(2)}, u32[]{:S(2)}) %collective-permute-start.3) | collective-permute-done | bytes 73760 | tf_op jit(solution)/shard_map/ppermute | solution.py:252
  39.8 1.3 collective-permute-start.6
  41.1 2.6 %collective-permute-start.4 = (f32[144,128]{1,0:T(8,128)S(1)}, f32[144,128]{1,0:T(8,128)S(1)}, u32[]{:S(2)}, u32[]{:S(2)}) collective-permute-start(f32[144,128]{1,0:T(8,128)S(1)} %add.33), channel_id=1, source_target_pairs={{0,2},{1,3},{2,0},{3,1},{4,6},{5,7},{6,4},{7,5},{8,10},{9,11},{10,... | collective-permute-start | bytes 221192 | tf_op jit(solution)/shard_map/ppermute | solution.py:252
  43.7 0.6 slice_bitcast_fusion.4
  44.3 2.3 %collective-permute-done.4 = f32[144,128]{1,0:T(8,128)S(1)} collective-permute-done((f32[144,128]{1,0:T(8,128)S(1)}, f32[144,128]{1,0:T(8,128)S(1)}, u32[]{:S(2)}, u32[]{:S(2)}) %collective-permute-start.4) | collective-permute-done | bytes 73760 | tf_op jit(solution)/shard_map/ppermute | solution.py:252
  46.6 0.6 add.34.total
  47.3 0.0 collective-permute-done.9.za
  47.3 0.0 collective-permute-done.8.zb
  47.3 0.0 collective-permute-done.6.xa
  47.3 0.5 copy-done.6
  47.9 0.0 copy-done.7
  47.9 0.1 copy-done
  47.9 0.0 copy-done.2
  48.0 19.5 %shard_map.42 = (f32[8,32,16,128]{3,2,1,0:T(8,128)}, bf16[8,32,16,128]{3,2,1,0:T(8,128)(2,1)}, bf16[32,16,128]{2,1,0:T(8,128)(2,1)}, bf16[32,16,128]{2,1,0:T(8,1...) custom-call(f32[2]{0:T(128)} %add_convert_fusion.flags_ref, f32[144,128]{1,0:T(8,128)} %add.34.total, ...), custom_call_target="tpu_custom_call" | custom-call | tf_op jit(solution)/shard_map/pallas_call | solution.py:276
  67.4 0.0 collective-permute-start.12
  67.5 1.3 collective-permute-start.14
  68.8 4.5 %collective-permute-start.13 = (bf16[8,16,128]{2,1,0:T(8,128)(2,1)}, bf16[8,16,128]{2,1,0:T(8,128)(2,1)S(1)}, u32[]{:S(2)}, u32[]{:S(2)}) collective-permute-start(bf16[8,16,128]{2,1,0:T(8,128)(2,1)} %get-tuple-element.33), channel_id=1, source_target_pairs={{0,1},{1,2},{2,3},{4,5},{5,6},{6,7},{8,9},{9,10},{10,11},{12,13},{... | collective-permute-start | bytes 98312 | tf_op jit(solution)/shard_map/ppermute | solution.py:261
  73.3 4.3 %collective-permute-start.10 = (bf16[32,16,128]{2,1,0:T(8,128)(2,1)}, bf16[32,16,128]{2,1,0:T(8,128)(2,1)S(1)}, u32[]{:S(2)}, u32[]{:S(2)}) collective-permute-start(bf16[32,16,128]{2,1,0:T(8,128)(2,1)} %get-tuple-element.30), channel_id=1, source_target_pairs={{0,8},{8,16},{16,24},{1,9},{9,17},{17,25},{2,10},{10,18},{18,26},{... | collective-permute-start | bytes 393224 | tf_op jit(solution)/shard_map/ppermute | solution.py:261
  77.7 1.3 collective-permute-start.11
  79.0 0.0 collective-permute-done.12
  79.0 0.6 slice_bitcast_fusion.2
  79.6 0.0 collective-permute-done.14.za
  79.6 0.0 collective-permute-done.13.zb
  79.6 1.2 collective-permute-done.10.xb
  80.8 4.5 %collective-permute-done.11.xa = bf16[32,16,128]{2,1,0:T(8,128)(2,1)S(1)} collective-permute-done((bf16[32,16,128]{2,1,0:T(8,128)(2,1)}, bf16[32,16,128]{2,1,0:T(8,128)(2,1)S(1)}, u32[]{:S(2)}, u32[]{:S(2)}) %collective-permute-start.11) | collective-permute-done | bytes 131104 | tf_op jit(solution)/shard_map/ppermute | solution.py:261
  85.3 0.6 copy-done.5
  85.9 17.3 %shard_map.43 = (bf16[8,32,16,128]{3,2,1,0:T(8,128)(2,1)}, bf16[32,16,128]{2,1,0:T(8,128)(2,1)}, bf16[32,16,128]{2,1,0:T(8,128)(2,1)}, bf16[2,8,16,128]{3,2,1,0:...) custom-call(f32[2]{0:T(128)} %add_convert_fusion.flags_ref, f32[8,32,16,128]{3,2,1,0:T(8,128)} %get-tuple-element.28.sc, ...), custom_call_target="tpu_custom_call" | custom-call | tf_op jit(solution)/shard_map/pallas_call | solution.py:276
  103.2 0.0 collective-permute-start.15
  103.2 1.5 collective-permute-done.15
  104.7 0.9 add.35
  105.6 1.8 %collective-permute-start.16 = (f32[144,128]{1,0:T(8,128)S(1)}, f32[144,128]{1,0:T(8,128)S(1)}, u32[]{:S(2)}, u32[]{:S(2)}) collective-permute-start(f32[144,128]{1,0:T(8,128)S(1)} %add.35), channel_id=1, source_target_pairs={{0,8},{8,0},{16,24},{24,16},{1,9},{9,1},{17,25},{25,17},{2,10},{10... | collective-permute-start | bytes 221192 | tf_op jit(solution)/shard_map/ppermute | solution.py:252
  107.4 2.6 %collective-permute-done.16 = f32[144,128]{1,0:T(8,128)S(1)} collective-permute-done((f32[144,128]{1,0:T(8,128)S(1)}, f32[144,128]{1,0:T(8,128)S(1)}, u32[]{:S(2)}, u32[]{:S(2)}) %collective-permute-start.16) | collective-permute-done | bytes 73760 | tf_op jit(solution)/shard_map/ppermute | solution.py:252
  110.0 0.1 collective-permute-start.17
  110.1 4.3 %collective-permute-done.17 = f32[144,128]{1,0:T(8,128)S(1)} collective-permute-done((f32[144,128]{1,0:T(8,128)S(1)}, f32[144,128]{1,0:T(8,128)S(1)}, u32[]{:S(2)}, u32[]{:S(2)}) %collective-permute-start.17) | collective-permute-done | bytes 73760 | tf_op jit(solution)/shard_map/ppermute | solution.py:252
  114.4 1.7 %collective-permute-start.18 = (f32[144,128]{1,0:T(8,128)S(1)}, f32[144,128]{1,0:T(8,128)S(1)}, u32[]{:S(2)}, u32[]{:S(2)}) collective-permute-start(f32[144,128]{1,0:T(8,128)S(1)} %add.37), channel_id=1, source_target_pairs={{0,1},{1,0},{2,3},{3,2},{4,5},{5,4},{6,7},{7,6},{8,9},{9,8},{10,11... | collective-permute-start | bytes 221192 | tf_op jit(solution)/shard_map/ppermute | solution.py:252
  116.1 1.3 collective-permute-start.24
  117.4 4.5 %collective-permute-start.23 = (bf16[8,16,128]{2,1,0:T(8,128)(2,1)}, bf16[8,16,128]{2,1,0:T(8,128)(2,1)S(1)}, u32[]{:S(2)}, u32[]{:S(2)}) collective-permute-start(bf16[8,16,128]{2,1,0:T(8,128)(2,1)} %get-tuple-element.39), channel_id=1, source_target_pairs={{0,1},{1,2},{2,3},{4,5},{5,6},{6,7},{8,9},{9,10},{10,11},{12,13},{... | collective-permute-start | bytes 98312 | tf_op jit(solution)/shard_map/ppermute | solution.py:261
  122.0 3.7 %collective-permute-start.20 = (bf16[32,16,128]{2,1,0:T(8,128)(2,1)}, bf16[32,16,128]{2,1,0:T(8,128)(2,1)S(1)}, u32[]{:S(2)}, u32[]{:S(2)}) collective-permute-start(bf16[32,16,128]{2,1,0:T(8,128)(2,1)} %get-tuple-element.36), channel_id=1, source_target_pairs={{0,8},{8,16},{16,24},{1,9},{9,17},{17,25},{2,10},{10,18},{18,26},{... | collective-permute-start | bytes 393224 | tf_op jit(solution)/shard_map/ppermute | solution.py:261
  125.7 1.3 collective-permute-start.21
  127.0 1.2 collective-permute-start.19
  128.2 0.6 slice_bitcast_fusion
  128.8 4.4 %collective-permute-done.19 = f32[144,128]{1,0:T(8,128)S(1)} collective-permute-done((f32[144,128]{1,0:T(8,128)S(1)}, f32[144,128]{1,0:T(8,128)S(1)}, u32[]{:S(2)}, u32[]{:S(2)}) %collective-permute-start.19) | collective-permute-done | bytes 73760 | tf_op jit(solution)/shard_map/ppermute | solution.py:252
  133.2 0.6 add.39.total
  133.8 0.0 collective-permute-done.24.za
  133.8 0.0 collective-permute-done.23.zb
  133.9 0.0 collective-permute-done.21.xa
  133.9 0.6 copy-done.8
  134.5 0.1 copy-done.1
  134.5 0.0 copy-done.3
  134.6 17.4 %shard_map.44 = (bf16[16,8,32,128]{3,2,1,0:T(8,128)(2,1)}, f32[16,32]{1,0:T(8,128)}) custom-call(f32[2]{0:T(128)} %add_convert_fusion.flags_ref, f32[144,128]{1,0:T(8,128)} %add.39.total, bf16[8,32,32,128]{3,2,1,0:T(8,128)(2,1)} %get-tuple-element.22.xt, bf16[8,32,16,128]{3,2,1,0:T(8,128)(2,1)} %get-tuple-element.35.qt, bf16[32,16,128]{2,1,0:T(8,128)(2,1)} %copy-done.1, ...), custom_call_target="tpu_custom_call" | custom-call | tf_op jit(solution)/shard_map/pallas_call | solution.py:276
  (28 shorter events, 0.1 us)
Async XLA Ops:
  16.1 1.6 %collective-permute-start = (f32[144,128]{1,0:T(8,128)}, f32[144,128]{1,0:T(8,128)S(1)}, u32[]{:S(2)}, u32[]{:S(2)}) collective-permute-start(f32[144,128]{1,0:T(8,128)} %get-tuple-element.21), channel_id=1, source_target_pairs={{0,4},{4,0},{1,5},{5,1},{2,6},{6,2},{3,7},{7,3},{8,12},{12,8},{9,1... | collective-permute-start | bytes 221192 | tf_op jit(solution)/shard_map/ppermute | solution.py:252
  18.6 5.5 %collective-permute-start.1 = (f32[144,128]{1,0:T(8,128)S(1)}, f32[144,128]{1,0:T(8,128)S(1)}, u32[]{:S(2)}, u32[]{:S(2)}) collective-permute-start(f32[144,128]{1,0:T(8,128)S(1)} %add.30), channel_id=1, source_target_pairs={{0,8},{8,0},{16,24},{24,16},{1,9},{9,1},{17,25},{25,17},{2,10},{10... | collective-permute-start | bytes 221192 | tf_op jit(solution)/shard_map/ppermute | solution.py:252
  24.1 11.2 %collective-permute-start.2 = (f32[144,128]{1,0:T(8,128)S(1)}, f32[144,128]{1,0:T(8,128)S(1)}, u32[]{:S(2)}, u32[]{:S(2)}) collective-permute-start(f32[144,128]{1,0:T(8,128)S(1)} %add.31), channel_id=1, source_target_pairs={{0,16},{8,24},{16,0},{24,8},{1,17},{9,25},{17,1},{25,9},{2,18},{10... | collective-permute-start | bytes 221192 | tf_op jit(solution)/shard_map/ppermute | solution.py:252
  25.9 21.3 %collective-permute-start.9 = (bf16[8,16,128]{2,1,0:T(8,128)(2,1)}, bf16[8,16,128]{2,1,0:T(8,128)(2,1)S(1)}, u32[]{:S(2)}, u32[]{:S(2)}) collective-permute-start(bf16[8,16,128]{2,1,0:T(8,128)(2,1)} %get-tuple-element.27), channel_id=1, source_target_pairs={{1,0},{2,1},{3,2},{5,4},{6,5},{7,6},{9,8},{10,9},{11,10},{13,12},{... | collective-permute-start | bytes 98312 | tf_op jit(solution)/shard_map/ppermute | solution.py:261
  27.2 20.0 %collective-permute-start.8 = (bf16[8,16,128]{2,1,0:T(8,128)(2,1)}, bf16[8,16,128]{2,1,0:T(8,128)(2,1)S(1)}, u32[]{:S(2)}, u32[]{:S(2)}) collective-permute-start(bf16[8,16,128]{2,1,0:T(8,128)(2,1)} %get-tuple-element.27), channel_id=1, source_target_pairs={{0,1},{1,2},{2,3},{4,5},{5,6},{6,7},{8,9},{9,10},{10,11},{12,13},{... | collective-permute-start | bytes 98312 | tf_op jit(solution)/shard_map/ppermute | solution.py:261
  31.8 9.3 %collective-permute-start.7 = (bf16[2,8,16,128]{3,2,1,0:T(8,128)(2,1)}, bf16[2,8,16,128]{3,2,1,0:T(8,128)(2,1)S(1)}, u32[]{:S(2)}, u32[]{:S(2)}) collective-permute-start(bf16[2,8,16,128]{3,2,1,0:T(8,128)(2,1)} %get-tuple-element.26), channel_id=1, source_target_pairs={{0,4},{4,0},{1,5},{5,1},{2,6},{6,2},{3,7},{7,3},{8,12},{12,8},{9,1... | collective-permute-start | bytes 196616 | tf_op jit(solution)/shard_map/ppermute | solution.py:265
  31.9 15.4 %collective-permute-start.5 = (bf16[32,16,128]{2,1,0:T(8,128)(2,1)}, bf16[32,16,128]{2,1,0:T(8,128)(2,1)S(1)}, u32[]{:S(2)}, u32[]{:S(2)}) collective-permute-start(bf16[32,16,128]{2,1,0:T(8,128)(2,1)} %get-tuple-element.24), channel_id=1, source_target_pairs={{0,8},{8,16},{16,24},{1,9},{9,17},{17,25},{2,10},{10,18},{18,26},{... | collective-permute-start | bytes 393224 | tf_op jit(solution)/shard_map/ppermute | solution.py:261
  35.3 4.4 %collective-permute-start.3 = (f32[144,128]{1,0:T(8,128)S(1)}, f32[144,128]{1,0:T(8,128)S(1)}, u32[]{:S(2)}, u32[]{:S(2)}) collective-permute-start(f32[144,128]{1,0:T(8,128)S(1)} %add.32), channel_id=1, source_target_pairs={{0,1},{1,0},{2,3},{3,2},{4,5},{5,4},{6,7},{7,6},{8,9},{9,8},{10,11... | collective-permute-start | bytes 221192 | tf_op jit(solution)/shard_map/ppermute | solution.py:252
  39.8 7.5 %collective-permute-start.6 = (bf16[32,16,128]{2,1,0:T(8,128)(2,1)}, bf16[32,16,128]{2,1,0:T(8,128)(2,1)S(1)}, u32[]{:S(2)}, u32[]{:S(2)}) collective-permute-start(bf16[32,16,128]{2,1,0:T(8,128)(2,1)} %get-tuple-element.25), channel_id=1, source_target_pairs={{8,0},{16,8},{24,16},{9,1},{17,9},{25,17},{10,2},{18,10},{26,18},{... | collective-permute-start | bytes 393224 | tf_op jit(solution)/shard_map/ppermute | solution.py:261
  41.1 5.5 %collective-permute-start.4 = (f32[144,128]{1,0:T(8,128)S(1)}, f32[144,128]{1,0:T(8,128)S(1)}, u32[]{:S(2)}, u32[]{:S(2)}) collective-permute-start(f32[144,128]{1,0:T(8,128)S(1)} %add.33), channel_id=1, source_target_pairs={{0,2},{1,3},{2,0},{3,1},{4,6},{5,7},{6,4},{7,5},{8,10},{9,11},{10,... | collective-permute-start | bytes 221192 | tf_op jit(solution)/shard_map/ppermute | solution.py:252
  47.3 0.6 copy-start.6
  47.3 0.6 copy-start.7
  47.3 0.7 copy-start
  47.3 0.7 copy-start.2
  67.4 11.5 %collective-permute-start.12 = (bf16[2,8,16,128]{3,2,1,0:T(8,128)(2,1)}, bf16[2,8,16,128]{3,2,1,0:T(8,128)(2,1)S(1)}, u32[]{:S(2)}, u32[]{:S(2)}) collective-permute-start(bf16[2,8,16,128]{3,2,1,0:T(8,128)(2,1)} %get-tuple-element.32), channel_id=1, source_target_pairs={{0,4},{4,0},{1,5},{5,1},{2,6},{6,2},{3,7},{7,3},{8,12},{12,8},{9,1... | collective-permute-start | bytes 196616 | tf_op jit(solution)/shard_map/ppermute | solution.py:265
  67.5 12.1 %collective-permute-start.14 = (bf16[8,16,128]{2,1,0:T(8,128)(2,1)}, bf16[8,16,128]{2,1,0:T(8,128)(2,1)S(1)}, u32[]{:S(2)}, u32[]{:S(2)}) collective-permute-start(bf16[8,16,128]{2,1,0:T(8,128)(2,1)} %get-tuple-element.33), channel_id=1, source_target_pairs={{1,0},{2,1},{3,2},{5,4},{6,5},{7,6},{9,8},{10,9},{11,10},{13,12},{... | collective-permute-start | bytes 98312 | tf_op jit(solution)/shard_map/ppermute | solution.py:261
  68.8 10.8 %collective-permute-start.13 = (bf16[8,16,128]{2,1,0:T(8,128)(2,1)}, bf16[8,16,128]{2,1,0:T(8,128)(2,1)S(1)}, u32[]{:S(2)}, u32[]{:S(2)}) collective-permute-start(bf16[8,16,128]{2,1,0:T(8,128)(2,1)} %get-tuple-element.33), channel_id=1, source_target_pairs={{0,1},{1,2},{2,3},{4,5},{5,6},{6,7},{8,9},{9,10},{10,11},{12,13},{... | collective-permute-start | bytes 98312 | tf_op jit(solution)/shard_map/ppermute | solution.py:261
  73.3 7.5 %collective-permute-start.10 = (bf16[32,16,128]{2,1,0:T(8,128)(2,1)}, bf16[32,16,128]{2,1,0:T(8,128)(2,1)S(1)}, u32[]{:S(2)}, u32[]{:S(2)}) collective-permute-start(bf16[32,16,128]{2,1,0:T(8,128)(2,1)} %get-tuple-element.30), channel_id=1, source_target_pairs={{0,8},{8,16},{16,24},{1,9},{9,17},{17,25},{2,10},{10,18},{18,26},{... | collective-permute-start | bytes 393224 | tf_op jit(solution)/shard_map/ppermute | solution.py:261
  77.7 7.6 %collective-permute-start.11 = (bf16[32,16,128]{2,1,0:T(8,128)(2,1)}, bf16[32,16,128]{2,1,0:T(8,128)(2,1)S(1)}, u32[]{:S(2)}, u32[]{:S(2)}) collective-permute-start(bf16[32,16,128]{2,1,0:T(8,128)(2,1)} %get-tuple-element.31), channel_id=1, source_target_pairs={{8,0},{16,8},{24,16},{9,1},{17,9},{25,17},{10,2},{18,10},{26,18},{... | collective-permute-start | bytes 393224 | tf_op jit(solution)/shard_map/ppermute | solution.py:261
  79.6 5.7 %copy-start.10 = (bf16[8,16,128]{2,1,0:T(8,128)(2,1)}, bf16[8,16,128]{2,1,0:T(8,128)(2,1)S(1)}, u32[]{:S(2)}) copy-start(bf16[8,16,128]{2,1,0:T(8,128)(2,1)S(1)} %collective-permute-done.14.za) | copy-start | bytes 98308
  79.6 5.7 %copy-start.11 = (bf16[8,16,128]{2,1,0:T(8,128)(2,1)}, bf16[8,16,128]{2,1,0:T(8,128)(2,1)S(1)}, u32[]{:S(2)}) copy-start(bf16[8,16,128]{2,1,0:T(8,128)(2,1)S(1)} %collective-permute-done.13.zb) | copy-start | bytes 98308
  80.8 4.5 %copy-start.4 = (bf16[32,16,128]{2,1,0:T(8,128)(2,1)}, bf16[32,16,128]{2,1,0:T(8,128)(2,1)S(1)}, u32[]{:S(2)}) copy-start(bf16[32,16,128]{2,1,0:T(8,128)(2,1)S(1)} %collective-permute-done.10.xb) | copy-start | bytes 393220
  85.3 0.7 copy-start.5
  103.2 1.5 collective-permute-start.15
  105.6 4.4 %collective-permute-start.16 = (f32[144,128]{1,0:T(8,128)S(1)}, f32[144,128]{1,0:T(8,128)S(1)}, u32[]{:S(2)}, u32[]{:S(2)}) collective-permute-start(f32[144,128]{1,0:T(8,128)S(1)} %add.35), channel_id=1, source_target_pairs={{0,8},{8,0},{16,24},{24,16},{1,9},{9,1},{17,25},{25,17},{2,10},{10... | collective-permute-start | bytes 221192 | tf_op jit(solution)/shard_map/ppermute | solution.py:252
  110.0 4.4 %collective-permute-start.17 = (f32[144,128]{1,0:T(8,128)S(1)}, f32[144,128]{1,0:T(8,128)S(1)}, u32[]{:S(2)}, u32[]{:S(2)}) collective-permute-start(f32[144,128]{1,0:T(8,128)S(1)} %add.36), channel_id=1, source_target_pairs={{0,16},{8,24},{16,0},{24,8},{1,17},{9,25},{17,1},{25,9},{2,18},{10... | collective-permute-start | bytes 221192 | tf_op jit(solution)/shard_map/ppermute | solution.py:252
  114.4 11.2 %collective-permute-start.18 = (f32[144,128]{1,0:T(8,128)S(1)}, f32[144,128]{1,0:T(8,128)S(1)}, u32[]{:S(2)}, u32[]{:S(2)}) collective-permute-start(f32[144,128]{1,0:T(8,128)S(1)} %add.37), channel_id=1, source_target_pairs={{0,1},{1,0},{2,3},{3,2},{4,5},{5,4},{6,7},{7,6},{8,9},{9,8},{10,11... | collective-permute-start | bytes 221192 | tf_op jit(solution)/shard_map/ppermute | solution.py:252
  116.1 10.8 %collective-permute-start.22 = (bf16[2,8,16,128]{3,2,1,0:T(8,128)(2,1)}, bf16[2,8,16,128]{3,2,1,0:T(8,128)(2,1)S(1)}, u32[]{:S(2)}, u32[]{:S(2)}) collective-permute-start(bf16[2,8,16,128]{3,2,1,0:T(8,128)(2,1)} %get-tuple-element.38), channel_id=1, source_target_pairs={{0,4},{4,0},{1,5},{5,1},{2,6},{6,2},{3,7},{7,3},{8,12},{12,8},{9,1... | collective-permute-start | bytes 196616 | tf_op jit(solution)/shard_map/ppermute | solution.py:265
  116.1 17.7 %collective-permute-start.24 = (bf16[8,16,128]{2,1,0:T(8,128)(2,1)}, bf16[8,16,128]{2,1,0:T(8,128)(2,1)S(1)}, u32[]{:S(2)}, u32[]{:S(2)}) collective-permute-start(bf16[8,16,128]{2,1,0:T(8,128)(2,1)} %get-tuple-element.39), channel_id=1, source_target_pairs={{1,0},{2,1},{3,2},{5,4},{6,5},{7,6},{9,8},{10,9},{11,10},{13,12},{... | collective-permute-start | bytes 98312 | tf_op jit(solution)/shard_map/ppermute | solution.py:261
  117.4 16.4 %collective-permute-start.23 = (bf16[8,16,128]{2,1,0:T(8,128)(2,1)}, bf16[8,16,128]{2,1,0:T(8,128)(2,1)S(1)}, u32[]{:S(2)}, u32[]{:S(2)}) collective-permute-start(bf16[8,16,128]{2,1,0:T(8,128)(2,1)} %get-tuple-element.39), channel_id=1, source_target_pairs={{0,1},{1,2},{2,3},{4,5},{5,6},{6,7},{8,9},{9,10},{10,11},{12,13},{... | collective-permute-start | bytes 98312 | tf_op jit(solution)/shard_map/ppermute | solution.py:261
  122.0 11.9 %collective-permute-start.20 = (bf16[32,16,128]{2,1,0:T(8,128)(2,1)}, bf16[32,16,128]{2,1,0:T(8,128)(2,1)S(1)}, u32[]{:S(2)}, u32[]{:S(2)}) collective-permute-start(bf16[32,16,128]{2,1,0:T(8,128)(2,1)} %get-tuple-element.36), channel_id=1, source_target_pairs={{0,8},{8,16},{16,24},{1,9},{9,17},{17,25},{2,10},{10,18},{18,26},{... | collective-permute-start | bytes 393224 | tf_op jit(solution)/shard_map/ppermute | solution.py:261
  125.7 8.2 %collective-permute-start.21 = (bf16[32,16,128]{2,1,0:T(8,128)(2,1)}, bf16[32,16,128]{2,1,0:T(8,128)(2,1)S(1)}, u32[]{:S(2)}, u32[]{:S(2)}) collective-permute-start(bf16[32,16,128]{2,1,0:T(8,128)(2,1)} %get-tuple-element.37), channel_id=1, source_target_pairs={{8,0},{16,8},{24,16},{9,1},{17,9},{25,17},{10,2},{18,10},{26,18},{... | collective-permute-start | bytes 393224 | tf_op jit(solution)/shard_map/ppermute | solution.py:261
  127.0 6.2 %collective-permute-start.19 = (f32[144,128]{1,0:T(8,128)S(1)}, f32[144,128]{1,0:T(8,128)S(1)}, u32[]{:S(2)}, u32[]{:S(2)}) collective-permute-start(f32[144,128]{1,0:T(8,128)S(1)} %add.38), channel_id=1, source_target_pairs={{0,2},{1,3},{2,0},{3,1},{4,6},{5,7},{6,4},{7,5},{8,10},{9,11},{10,... | collective-permute-start | bytes 221192 | tf_op jit(solution)/shard_map/ppermute | solution.py:252
  133.8 0.6 copy-start.8
  133.8 0.6 copy-start.9
  133.9 0.7 copy-start.1
  133.9 0.7 copy-start.3

commit v2 on v0

v2 whole, which is shorter than its diff:
```python
import jax
import jax.numpy as jnp
from jax import lax
from jax.experimental import pallas as pl
from jax.experimental.pallas import tpu as pltpu
from jax.sharding import PartitionSpec as P

BETA = 1.0
RIDGE = 0.1
AXES = ("gx", "gy", "gz")
ROWS_ROWS = (((1,), (1,)), ((), ()))
VMEM_BYTES = 36 * 2**20
PIVOTS = 8
UNROLL = 2
f32, bf16 = jnp.float32, jnp.bfloat16


def iota(shape, dim):
    return lax.broadcasted_iota(jnp.int32, shape, dim)


def half_rows(feats, classes):
    return -(-(feats * feats * classes // 128 + feats + 8) // 16) * 8


def moments_of(x, q, chunk=8):
    ny, feats, _ = x.shape
    scatter = first = None
    for c in range(0, ny, chunk):
        xs = jnp.concatenate([x[y] for y in range(c, c + chunk)], axis=1)
        qs = jnp.concatenate([q[y] for y in range(c, c + chunk)], axis=1)
        weighted = jnp.concatenate([xs[f : f + 1] * qs for f in range(feats)], axis=0)
        ones = jnp.ones((16, xs.shape[1]), bf16)
        s = lax.dot_general(xs, weighted, ROWS_ROWS, preferred_element_type=f32)
        m = lax.dot_general(
            jnp.concatenate([xs, ones], axis=0), qs, ROWS_ROWS, preferred_element_type=f32
        )
        scatter = s if scatter is None else scatter + s
        first = m if first is None else first + m
    return scatter, first


def no_moments(feats, classes):
    return jnp.zeros((feats, feats * classes), f32), jnp.zeros((feats + 16, classes), f32)


def put_moments(place_ref, mine, theirs, scatter, first):
    feats, lanes = scatter.shape
    rows = [scatter[:, j : j + 128] for j in range(0, lanes, 128)]
    rows.append(jnp.pad(first[: feats + 8], ((0, 0), (0, 128 - first.shape[1]))))
    half = mine.shape[0]
    rows.append(jnp.zeros((2 * half - sum(r.shape[0] for r in rows), 128), f32))
    rows = jnp.concatenate(rows, axis=0)
    odd = Place(place_ref, 1).sends == 1
    mine[...] = jnp.where(odd, rows[half:], rows[:half])
    theirs[pl.ds(0, half), :] = jnp.where(odd, rows[:half], rows[half:])


def all_moments(place_ref, mine, theirs):
    odd = Place(place_ref, 1).sends == 1
    mine, theirs = mine[...], theirs[...]
    return jnp.concatenate([jnp.where(odd, theirs, mine), jnp.where(odd, mine, theirs)], axis=0)


def m_step(total, w_ref, bias_ref):
    classes = bias_ref.shape[0]
    feats = w_ref.shape[0] // classes
    groups = 128 // classes
    tiles = feats // groups
    lane, sub = iota((8, 128), 1), iota((8, 128), 0)
    group = lane // classes

    def rows(r):
        return total[r : r + 8]

    def spread_lanes(v, g):
        return jnp.take_along_axis(v, lane % classes + g * classes, axis=1, mode="promise_in_bounds")

    def spread_row(v, r):
        return jnp.broadcast_to(v[r : r + 1], (8, 128))

    base = tiles * feats
    counts = spread_lanes(spread_row(rows(base + feats), 0), 0)
    inv = 1.0 / counts
    means = [spread_lanes(rows(base + 8 * j), 0) / counts for j in range(tiles)]
    eye = jnp.where(sub == group, 1.0, 0.0)
    zero = jnp.zeros((8, 128), f32)
    mean_row = [
        jnp.broadcast_to(jnp.sum(eye * m, axis=0, keepdims=True), (8, 128)) for m in means
    ]
    mat = [
        [rows(t * feats + 8 * j) * inv - means[j] * mean_row[t] + (RIDGE * eye if t == j else 0.0) for t in range(tiles)]
        for j in range(tiles)
    ]
    side = [[eye if t == j else zero for t in range(tiles)] for j in range(tiles)] + [mean_row]
    diag = [zero] * tiles
    for p in range(0, feats, PIVOTS):
        at, g0 = p // 8, p % 8
        cols = [("m", j) for j in range(at, tiles)] + [("s", j) for j in (*range(at + 1), tiles)]
        held = {"m": mat, "s": side}
        head = [{(n, j): spread_lanes(held[n][j][at], g0 + s) for n, j in cols} for s in range(PIVOTS)]
        e = [[spread_row(head[s]["m", at], g0 + t) for t in range(PIVOTS)] for s in range(PIVOTS)]
        factors = [
            [spread_row(mat[at][t], g0 + s) if t >= at else None for t in range(tiles)] for s in range(PIVOTS)
        ]
        ells, scaled = {}, []
        for s in range(PIVOTS):
            r = 1.0 / e[s][s]
            for t in range(s + 1, PIVOTS):
                ells[s, t] = e[s][t] * r
                for c in cols:
                    head[t][c] = head[t][c] - ells[s, t] * head[s][c]
                for u in range(t, PIVOTS):
                    e[t][u] = e[t][u] - ells[s, t] * e[s][u]
            scaled.append({c: head[s][c] * r for c in cols})
        for s in reversed(range(PIVOTS)):
            for t in range(s + 1, PIVOTS):
                for c in cols:
                    scaled[s][c] = scaled[s][c] - ells[s, t] * scaled[t][c]
        for t in range(at, tiles):
            for s in range(PIVOTS):
                factor = factors[s][t]
                if t == at:
                    factor = jnp.where(group >= g0 + PIVOTS, factor, 0.0)
                for n, j in cols:
                    held[n][j][t] = held[n][j][t] - factor * scaled[s][n, j]
        for s in range(PIVOTS):
            own = group == g0 + s
            for n, j in cols:
                if n == "s":
                    side[j][at] = jnp.where(own, head[s][n, j], side[j][at])
            diag[at] = jnp.where(own, e[s][s], diag[at])
    logdet = sum(jnp.log(d) for d in diag)
    step = classes
    while step < 128:
        logdet = logdet + pltpu.roll(logdet, step, 1)
        step *= 2
    everything = jnp.sum(counts, axis=1, keepdims=True) * (1.0 / groups)
    bias = jnp.log(counts / everything) - 0.5 * logdet
    for t in range(tiles):
        scale = lax.rsqrt(diag[t])
        shift = -side[tiles][t] * scale
        high = shift.astype(bf16).astype(f32)
        middle = (shift - high).astype(bf16).astype(f32)
        low = shift - high - middle
        parts = jnp.where(sub == 0, high, jnp.where(sub == 1, middle, jnp.where(sub == 2, low, 0.0)))
        block = [side[j][t] * scale for j in range(tiles)] + [parts, zero, bias]
        turned = jnp.concatenate(block + [zero] * (16 - len(block)), axis=0).T
        w_ref[pl.ds(t * 128, 128), :] = turned[:, : feats + 16].astype(bf16)
        if t == 0:
            bias_ref[...] = jnp.broadcast_to(turned[:classes, feats + 16 : feats + 17], (classes, 128))
    return means


def loglik_of(x, w_ref, bias):
    n, feats, nz = x.shape
    classes = bias.shape[0]
    xs = jnp.concatenate([x[j] for j in range(n)], axis=1)
    xs = jnp.concatenate([xs, jnp.ones((16, n * nz), bf16)], axis=0)
    white = jnp.dot(w_ref[...], xs, preferred_element_type=f32)
    white = white * white
    square = white[:classes]
    for g in range(1, feats):
        square = square + white[g * classes : (g + 1) * classes]
    return jnp.stack(
        [bias[:, :nz] - 0.5 * square[:, j * nz : (j + 1) * nz] for j in range(n)], axis=0
    )


def sharing(ny):
    return 128 // (2 * ny)


def own_lane(i, nx, ny, classes):
    start = 2 * ny * (i // (nx // sharing(ny)))
    lane, y = iota((ny, classes, 128), 2), iota((ny, classes, 128), 0)
    return (lane == start + y) | (lane == start + ny + y)


def shift_matrix(ny, nz):
    src, dst = iota((nz + 128, nz), 0), iota((nz + 128, nz), 1)
    near = (src < nz) & ((src == dst + 1) | (src == dst - 1))
    face = src - nz
    first = face % (2 * ny) < ny
    edge = (face >= 0) & ((first & (dst == nz - 1)) | (jnp.logical_not(first) & (dst == 0)))
    return jnp.where(near | edge, 1.0, 0.0).astype(bf16)


def take_matrix(ny, nz):
    src, dst = iota((nz, 128), 0), iota((nz, 128), 1)
    first = dst % (2 * ny) < ny
    hit = ((src == 0) & first) | ((src == nz - 1) & jnp.logical_not(first))
    return jnp.where(hit, 1.0, 0.0).astype(bf16)


def near_of(i, q_ref, y_halo, z_halo):
    nx, ny, classes, nz = q_ref.shape
    nx = nx - 2
    mid = q_ref[i + 1]
    down = q_ref[i].astype(f32)
    up = q_ref[i + 2].astype(f32)
    mid32 = mid.astype(f32)
    left = jnp.concatenate([y_halo[0, pl.ds(i, 1)], mid32[:-1]], axis=0)
    right = jnp.concatenate([mid32[1:], y_halo[1, pl.ds(i, 1)]], axis=0)
    face = z_halo[i % (nx // sharing(ny))]
    face = jnp.where(own_lane(i, nx, ny, classes), face[None], 0.0).astype(bf16)
    both = jnp.concatenate([mid, face], axis=2).reshape(ny * classes, nz + 128)
    along = jnp.dot(both, shift_matrix(ny, nz), preferred_element_type=f32)
    return (down + up) + (left + right) + along.reshape(ny, classes, nz)


def update_of(scores, near):
    s = scores + BETA * near
    e = jnp.exp(s - jnp.max(s, axis=1, keepdims=True))
    return (e * (1.0 / jnp.sum(e, axis=1, keepdims=True))).astype(bf16)


class Place:
    def __init__(self, place_ref, axis):
        self.sends, self.gets, self.before, self.after = (place_ref[4 * axis + j] for j in range(4))

    def halo(self, inner, outer):
        before = jnp.where(self.gets == 1, inner, outer)
        after = jnp.where(self.gets == 1, outer, inner)
        before = jnp.where(self.before == 1, before, 0.0)
        after = jnp.where(self.after == 1, after, 0.0)
        return before, after


def fill_halo(place_ref, halo, q_ref, padded, y_halo, z_halo):
    xi, xo, yi, yo, zi, zo = halo
    nx, ny, classes, nz = q_ref.shape
    before, after = Place(place_ref, 0).halo(xi[...].astype(f32), xo[...].astype(f32))
    padded[0], padded[nx + 1] = before.astype(bf16), after.astype(bf16)
    for i in range(nx):
        padded[i + 1] = q_ref[i]
    rows = y_halo.shape[1] * classes
    before, after = Place(place_ref, 1).halo(*(y[pl.ds(y.shape[0] - rows, rows), :] for y in (yi, yo)))
    y_halo[0], y_halo[1] = before.reshape(y_halo.shape[1:]), after.reshape(y_halo.shape[1:])
    rows = z_halo.shape[0] * classes
    before, after = Place(place_ref, 2).halo(*(z[pl.ds(z.shape[0] - rows, rows), :] for z in (zi, zo)))
    first = iota(before.shape, 1) % (2 * ny) < ny
    z_halo[...] = jnp.where(first, after, before).reshape(z_halo.shape)


def put_faces(place_ref, i, q, xin, xout, yin, yout, zface):
    ny, classes, nz = q.shape
    nx = yout.shape[0] // classes
    sends_x, sends_y = Place(place_ref, 0).sends, Place(place_ref, 1).sends

    @pl.when(((i == 0) & (sends_x == 1)) | ((i == nx - 1) & (sends_x == 0)))
    def _():
        xin[...] = q

    @pl.when(((i == 0) & (sends_x == 0)) | ((i == nx - 1) & (sends_x == 1)))
    def _():
        xout[...] = q

    first, last = q[0].astype(f32), q[ny - 1].astype(f32)
    yin[pl.ds(yin.shape[0] - yout.shape[0] + i * classes, classes), :] = jnp.where(sends_y == 1, first, last)
    yout[pl.ds(i * classes, classes), :] = jnp.where(sends_y == 1, last, first)
    spread = jnp.dot(q.reshape(ny * classes, nz), take_matrix(ny, nz), preferred_element_type=f32)
    spread = jnp.where(own_lane(i, nx, ny, classes), spread.reshape(ny, classes, 128), 0.0)
    spread = jnp.sum(spread, axis=0)
    share = nx // sharing(ny)
    at = pl.ds((i % share) * classes, classes)
    zface[at, :] = jnp.where(i < share, spread, zface[at, :] + spread)


def first_kernel(
    place, x_hbm, q_hbm, xt, qt, xin, xout, yout, zface, mine, theirs, x_in, q_in, sems
):
    nx, ny, feats, nz = xt.shape
    classes = qt.shape[2]

    def copies(i):
        return (
            pltpu.make_async_copy(q_hbm.at[:, i], q_in.at[i], sems.at[0, i]),
            pltpu.make_async_copy(x_hbm.at[:, i], x_in.at[i], sems.at[1, i]),
        )

    for i in range(nx):
        for copy in copies(i):
            copy.start()

    zface[...] = jnp.zeros_like(zface)

    def slab(i, sums):
        for copy in copies(i):
            copy.wait()
        x = jnp.swapaxes(x_in[i], 0, 1)
        q = jnp.swapaxes(q_in[i], 0, 1)
        xt[i] = x
        qt[i] = q
        put_faces(place, i, q, xin, xout, theirs, yout, zface)
        return jax.tree.map(jnp.add, sums, moments_of(x, q))

    sums = lax.fori_loop(0, nx, slab, no_moments(feats, classes), unroll=UNROLL)
    put_moments(place, mine, theirs, *sums)


def second_kernel(
    place, mine, theirs, xt, qt, xi, xo, yi, yo, zi, zo, sc, q1, xin, xout, yin, yout, zface, w, bias, *space
):
    nx, ny = xt.shape[:2]
    fill_halo(place, (xi, xo, yi, yo, zi, zo), qt, *space)
    m_step(all_moments(place, mine, theirs), w, bias)
    zface[...] = jnp.zeros_like(zface)

    def slab(i, carry):
        half = ny // 2
        sc[i, pl.ds(0, half)] = loglik_of(xt[i, pl.ds(0, half)], w, bias[...])
        sc[i, pl.ds(half, half)] = loglik_of(xt[i, pl.ds(half, half)], w, bias[...])
        q = update_of(sc[i], near_of(i, *space))
        q1[i] = q
        put_faces(place, i, q, xin, xout, yin, yout, zface)
        return carry

    lax.fori_loop(0, nx, slab, 0, unroll=UNROLL)


def third_kernel(place, sc, xt, qt, xi, xo, yi, yo, zi, zo, q2, xin, xout, yout, zface, mine, theirs, *space):
    nx, _, feats, _ = xt.shape
    classes = qt.shape[2]
    fill_halo(place, (xi, xo, yi, yo, zi, zo), qt, *space)
    zface[...] = jnp.zeros_like(zface)

    def slab(i, sums):
        q = update_of(sc[i], near_of(i, *space))
        q2[i] = q
        put_faces(place, i, q, xin, xout, theirs, yout, zface)
        return jax.tree.map(jnp.add, sums, moments_of(xt[i], q))

    sums = lax.fori_loop(0, nx, slab, no_moments(feats, classes), unroll=UNROLL)
    put_moments(place, mine, theirs, *sums)


def fourth_kernel(place, mine, theirs, xt, qt, xi, xo, yi, yo, zi, zo, seg, means_ref, w, bias, *space):
    nx, ny = xt.shape[:2]
    classes, feats = means_ref.shape
    fill_halo(place, (xi, xo, yi, yo, zi, zo), qt, *space)
    means = jnp.concatenate(m_step(all_moments(place, mine, theirs), w, bias), axis=0)
    means = jnp.concatenate([means, jnp.zeros((128 - feats, 128), f32)], axis=0).T
    means_ref[...] = means[:classes, :feats]

    def slab(i, carry):
        half = ny // 2
        scores = jnp.concatenate(
            [loglik_of(xt[i, pl.ds(j * half, half)], w, bias[...]) for j in range(2)], axis=0
        )
        q = update_of(scores, near_of(i, *space))
        seg[:, i] = jnp.swapaxes(q, 0, 1)
        return carry

    lax.fori_loop(0, nx, slab, 0, unroll=UNROLL)


def pairings(n):
    if n == 2:
        return [[1, 0]]
    if n == 4:
        return [[1, 0, 3, 2], [3, 2, 1, 0], [2, 3, 0, 1]]
    return None


def send(value, axis, to):
    return lax.ppermute(value, axis, list(enumerate(to)))


def place_along(axis):
    n, at = lax.axis_size(axis), lax.axis_index(axis)
    if pairings(n) is None:
        return [0 * at, 0 * at + 1, at > 0, at < n - 1]
    return [at % 2, at % 2, at > 0, at < n - 1]


def swap(axis, inner, outer):
    n = lax.axis_size(axis)
    if n == 2:
        got = send(inner, axis, [1, 0])
        return got, got
    if n == 4:
        return tuple(send(v, axis, to) for v, to in zip((inner, outer), pairings(n)))
    return send(inner, axis, [(i + 1) % n for i in range(n)]), send(outer, axis, [(i - 1) % n for i in range(n)])


def exchange(xin, xout, yin, yout, zface):
    return *swap("gx", xin, xout), *swap("gy", yin, yout), *swap("gz", zface, zface)


def sum_and_exchange(xin, xout, yout, zface, mine, theirs):
    rows = mine.shape[0]
    paired = lax.axis_size("gy") == 2
    if paired:
        yi = yo = send(theirs, "gy", [1, 0])
        total = mine + yi[:rows]
    else:
        yi, yo = swap("gy", theirs[rows:], yout)
        total = lax.psum(jnp.concatenate([mine, theirs[:rows]], axis=0), "gy")
    if lax.axis_size("gx") == 4:
        total = sum((send(total, "gx", to) for to in pairings(4)), total)
    else:
        total = lax.psum(total, "gx")
    total, xin, xout = lax.optimization_barrier((total, xin, xout))
    xi, xo = swap("gx", xin, xout)
    if lax.axis_size("gz") == 4:
        n = total.shape[0]
        both = jnp.concatenate([total, zface], axis=0)
        zi, zo = (send(both, "gz", to) for to in pairings(4)[:2])
        total = total + zi[:n] + zo[:n] + send(total, "gz", pairings(4)[2])
    else:
        zi, zo = swap("gz", zface, zface)
        total = lax.psum(total, "gz")
    total, xi, xo = lax.optimization_barrier((total, xi, xo))
    halves = (total, send(total, "gy", [1, 0])) if paired else (total[:rows], total[rows:])
    return *halves, xi, xo, yi, yo, zi, zo


def call(kernel, outs, scratch, places, *args, vmem=VMEM_BYTES):
    specs = [pl.BlockSpec(memory_space=place) for place in places]
    specs += [pl.BlockSpec(memory_space=pltpu.VMEM)] * (len(args) - len(places))
    return pl.pallas_call(
        kernel,
        out_shape=tuple(outs),
        in_specs=specs,
        out_specs=tuple(pl.BlockSpec(memory_space=pltpu.VMEM) for _ in outs),
        scratch_shapes=scratch,
        compiler_params=pltpu.CompilerParams(vmem_limit_bytes=vmem),
    )(*args)


def local(features, posteriors):
    feats, nx, ny, nz = features.shape
    classes = posteriors.shape[0]
    share = nx // sharing(ny)
    shape = jax.ShapeDtypeStruct
    brick = shape((nx, ny, classes, nz), bf16)
    face_x = shape((ny, classes, nz), bf16)
    face_y = shape((nx * classes, nz), f32)
    face_z = shape((share * classes, 128), f32)
    half = half_rows(feats, classes)
    mine, theirs = shape((half, 128), f32), shape((half + nx * classes, 128), f32)
    solved = [pltpu.VMEM((feats * classes, feats + 16), bf16), pltpu.VMEM((classes, 128), f32)]
    halos = [
        pltpu.VMEM((nx + 2, ny, classes, nz), bf16),
        pltpu.VMEM((2, nx, classes, nz), f32),
        pltpu.VMEM((share, classes, 128), f32),
    ]
    place = jnp.stack([jnp.asarray(v, jnp.int32) for axis in AXES for v in place_along(axis)])

    xt, qt, *edge = call(
        first_kernel,
        [shape((nx, ny, feats, nz), bf16), brick, face_x, face_x, face_y, face_z, mine, theirs],
        [
            pltpu.VMEM((nx, feats, ny, nz), bf16),
            pltpu.VMEM((nx, classes, ny, nz), bf16),
            pltpu.SemaphoreType.DMA((2, nx)),
        ],
        [pltpu.SMEM, pltpu.HBM, pltpu.HBM],
        place,
        features,
        posteriors,
        vmem=48 * 2**20,
    )
    *total, xi, xo, yi, yo, zi, zo = sum_and_exchange(*edge)
    halo = (xi, xo, yi, yo, zi, zo)
    sc, q1, *edge = call(
        second_kernel,
        [shape((nx, ny, classes, nz), f32), brick, face_x, face_x, face_y, face_y, face_z],
        solved + halos,
        [pltpu.SMEM],
        place,
        *total,
        xt,
        qt,
        *halo,
    )
    halo = exchange(*edge)
    q2, *edge = call(
        third_kernel,
        [brick, face_x, face_x, face_y, face_z, mine, theirs],
        halos,
        [pltpu.SMEM],
        place,
        sc,
        xt,
        q1,
        *halo,
    )
    *total, xi, xo, yi, yo, zi, zo = sum_and_exchange(*edge)
    halo = (xi, xo, yi, yo, zi, zo)
    return call(
        fourth_kernel,
        [shape(posteriors.shape, bf16), shape((classes, feats), f32)],
        solved + halos,
        [pltpu.SMEM],
        place,
        *total,
        xt,
        q2,
        *halo,
    )


def solution(mesh):
    placed = P(None, "gx", "gy", "gz")
    return jax.shard_map(
        local, mesh=mesh, in_specs=(placed, placed), out_specs=(placed, P()), check_vma=False
    )
```

time: 864 us -> 112 us (0.13); the launches traced: 853 us -> 111 us
  other arithmetic: 233 us -> 0.08 us
  matrix products: 182 us -> 0 us
  waiting for transfers between devices: 171 us -> 24.9 us
  local copies, waits for them, and re-layouts: 127 us -> 1.33 us
  blocking collectives: 81.6 us -> 0 us
  Pallas kernels: 0 us -> 56.2 us
  between operations: 15.2 us -> 0.76 us
  starting transfers between devices: 40.8 us -> 28 us
    dot_general x68 -> x0, matrix products: 180 us -> none  [the longest x32 93.2 us: second(): lax.dot_general(weighted, flat_vox, contract, preferred_element_type=jnp....]
    another operation x11 -> x0, other arithmetic: 173 us -> none  [the longest x7 94.1 us: finish(): factor = jnp.linalg.cholesky(spread)]
    psum x2 -> x0, waiting for transfers between devices: 159 us -> none  [fit(): lax.psum((counts, first_moment, scatter), ('gx', 'gy', 'gz'))]
    psum x2 -> x0, blocking collectives: 81.6 us -> none  [fit(): lax.psum((counts, first_moment, scatter), ('gx', 'gy', 'gz'))]
    pallas_call x0 -> x4, Pallas kernels: none -> 56.2 us  [call(): pl.pallas_call(kernel, out_shape=tuple(outs), in_specs=specs, out_specs=t...]
    dynamic_slice x64 -> x0, local copies, waits for them, and re-layouts: 33.4 us -> none  [the longest x32 20.2 us: loglik(): scores = lax.map(per_class, (rounded, offset, biases))]
    dynamic_update_slice x32 -> x0, local copies, waits for them, and re-layouts: 30.3 us -> none  [loglik(): scores = lax.map(per_class, (rounded, offset, biases))]
    sub x34 -> x0, other arithmetic: 21.8 us -> none  [the longest x32 19.9 us: per_class(): return level - 0.5 * jnp.sum(whitened * whitened, axis=0)]
  transfers between devices with their start and end apart: 20 -> 25, of which waited for: 8 -> 19; matrix products, arithmetic and copies ran while one was open for 50% -> 0% of each run, Pallas kernels for 0% -> 0%
where the time goes in v2:
time: 112 us; the launch traced here: 111 us
  Pallas kernels  56.2 us (50%)
  starting transfers between devices  28 us (25%)
  waiting for transfers between devices  24.9 us (22%)
  local copies, waits for them, and re-layouts  1.33 us (1%)
    pallas_call x4, Pallas kernels, call(): pl.pallas_call(kernel, out_shape=tuple(outs), in_specs=specs, out_specs=t...  56.2 us
    ppermute x25, starting transfers between devices, send(): return lax.ppermute(value, axis, list(enumerate(to)))  28 us
    ppermute x25, waiting for transfers between devices, send(): return lax.ppermute(value, axis, list(enumerate(to)))  24.9 us
  transfers between devices with their start and end apart: 25, of which 19 were waited for; matrix products, arithmetic and copies ran while one was open for 0% of the time, Pallas kernels for 0%

profile of v2, /device:TPU:0, one launch (start us, length us, event | category | flops | bytes accessed | tf_op | source)
XLA Modules:
  0.0 111.4 jit_solution(14096676691751280595)
XLA Ops:
  0.7 0.1 stack.66.place
  0.8 0.0 copy-start
  0.8 1.2 %copy-done = bf16[16,8,32,128]{3,2,1,0:T(8,128)(2,1)S(1)} copy-done((bf16[16,8,32,128]{3,2,1,0:T(8,128)(2,1)S(1)}, bf16[16,8,32,128]{3,2,1,0:T(8,128)(2,1)}, u32[]{:S(2)}) %copy-start) | copy-done | bytes 1048600
  2.0 13.7 %shard_map.41 = (bf16[8,32,32,128]{3,2,1,0:T(8,128)(2,1)S(1)}, bf16[8,32,16,128]{3,2,1,0:T(8,128)(2,1)S(1)}, bf16[32,16,128]{2,1,0:T(8,128)(2,1)S(1)}, bf16[32,1...) custom-call(s32[12]{0:T(128)S(1)} %stack.66.place, ...), custom_call_target="tpu_custom_call" | custom-call | tf_op jit(solution)/shard_map/pallas_call | solution.py:422
  15.7 0.5 collective-permute-start
  16.2 1.0 collective-permute-done.yi.yo
  17.2 2.9 %collective-permute-start.3 = (f32[88,128]{1,0:T(8,128)S(1)}, f32[88,128]{1,0:T(8,128)S(1)}, u32[]{:S(2)}, u32[]{:S(2)}) collective-permute-start(f32[88,128]{1,0:T(8,128)S(1)} %slice_add_fusion.5), channel_id=1, source_target_pairs={{0,16},{8,24},{16,0},{24,8},{1,17},{9,25},{17,1},{25,9},{2,18},{10... | collective-permute-start | bytes 135176 | tf_op jit(solution)/shard_map/ppermute | solution.py:367
  20.1 1.4 %collective-permute-start.2 = (f32[88,128]{1,0:T(8,128)S(1)}, f32[88,128]{1,0:T(8,128)S(1)}, u32[]{:S(2)}, u32[]{:S(2)}) collective-permute-start(f32[88,128]{1,0:T(8,128)S(1)} %slice_add_fusion.5), channel_id=1, source_target_pairs={{0,24},{8,16},{16,8},{24,0},{1,25},{9,17},{17,9},{25,1},{2,26},{10... | collective-permute-start | bytes 135176 | tf_op jit(solution)/shard_map/ppermute | solution.py:367
  21.5 0.1 collective-permute-start.1
  21.6 0.5 collective-permute-done.3
  22.2 3.3 %collective-permute-done.2 = f32[88,128]{1,0:T(8,128)S(1)} collective-permute-done((f32[88,128]{1,0:T(8,128)S(1)}, f32[88,128]{1,0:T(8,128)S(1)}, u32[]{:S(2)}, u32[]{:S(2)}) %collective-permute-start.2) | collective-permute-done | bytes 45088 | tf_op jit(solution)/shard_map/ppermute | solution.py:367
  25.5 0.1 collective-permute-done.1
  25.6 3.7 %collective-permute-start.5 = (f32[152,128]{1,0:T(8,128)S(1)}, f32[152,128]{1,0:T(8,128)S(1)}, u32[]{:S(2)}, u32[]{:S(2)}) collective-permute-start(f32[152,128]{1,0:T(8,128)S(1)} %constant_dynamic-update-slice_fusion), channel_id=1, source_target_pairs={{0,3},{1,2},{2,1},{3,0},{4,7},{5,6},{6,5},{7,4},{8,11},{9,10},{10,... | collective-permute-start | bytes 233480 | tf_op jit(solution)/shard_map/ppermute | solution.py:367
  29.3 0.0 collective-permute-start.4
  29.3 0.8 collective-permute-start.6
  30.1 1.0 collective-permute-start.7
  31.0 2.0 %collective-permute-start.8 = (bf16[32,16,128]{2,1,0:T(8,128)(2,1)S(1)}, bf16[32,16,128]{2,1,0:T(8,128)(2,1)S(1)}, u32[]{:S(2)}, u32[]{:S(2)}) collective-permute-start(bf16[32,16,128]{2,1,0:T(8,128)(2,1)S(1)} %get-tuple-element.40), channel_id=1, source_target_pairs={{0,24},{8,16},{16,8},{24,0},{1,25},{9,17},{17,9},{25,1},{2,26},{10... | collective-permute-start | bytes 393224 | tf_op jit(solution)/shard_map/ppermute | solution.py:367
  33.1 1.2 %collective-permute-done.6 = f32[88,128]{1,0:T(8,128)S(1)} collective-permute-done((f32[88,128]{1,0:T(8,128)S(1)}, f32[88,128]{1,0:T(8,128)S(1)}, u32[]{:S(2)}, u32[]{:S(2)}) %collective-permute-start.6) | collective-permute-done | bytes 45088 | tf_op jit(solution)/shard_map/ppermute | solution.py:367
  34.2 0.0 collective-permute-done.5.zo
  34.2 0.0 collective-permute-done.4.zi
  34.3 1.0 collective-permute-done.7.xi
  35.3 2.2 %collective-permute-done.8.xo = bf16[32,16,128]{2,1,0:T(8,128)(2,1)S(1)} collective-permute-done((bf16[32,16,128]{2,1,0:T(8,128)(2,1)S(1)}, bf16[32,16,128]{2,1,0:T(8,128)(2,1)S(1)}, u32[]{:S(2)}, u32[]{:S(2)}) %collective-permute-start.8) | collective-permute-done | bytes 131104 | tf_op jit(solution)/shard_map/ppermute | solution.py:367
  37.5 0.0 collective-permute-start.9
  37.5 1.2 %collective-permute-done.9.theirs = f32[88,128]{1,0:T(8,128)S(1)} collective-permute-done((f32[88,128]{1,0:T(8,128)S(1)}, f32[88,128]{1,0:T(8,128)S(1)}, u32[]{:S(2)}, u32[]{:S(2)}) %collective-permute-start.9) | collective-permute-done | bytes 45088 | tf_op jit(solution)/shard_map/ppermute | solution.py:367
  38.8 15.0 %shard_map.42 = (f32[8,32,16,128]{3,2,1,0:T(8,128)S(1)}, bf16[8,32,16,128]{3,2,1,0:T(8,128)(2,1)S(1)}, bf16[32,16,128]{2,1,0:T(8,128)(2,1)S(1)}, bf16[32,16,128]...) custom-call(s32[12]{0:T(128)S(1)} %stack.66.place, ...), custom_call_target="tpu_custom_call" | custom-call | tf_op jit(solution)/shard_map/pallas_call | solution.py:422
  53.7 0.4 collective-permute-start.10
  54.2 1.6 %collective-permute-start.11 = (bf16[32,16,128]{2,1,0:T(8,128)(2,1)S(1)}, bf16[32,16,128]{2,1,0:T(8,128)(2,1)S(1)}, u32[]{:S(2)}, u32[]{:S(2)}) collective-permute-start(bf16[32,16,128]{2,1,0:T(8,128)(2,1)S(1)} %get-tuple-element.49), channel_id=1, source_target_pairs={{0,24},{8,16},{16,8},{24,0},{1,25},{9,17},{17,9},{25,1},{2,26},{10... | collective-permute-start | bytes 393224 | tf_op jit(solution)/shard_map/ppermute | solution.py:367
  55.8 0.0 collective-permute-start.12
  55.8 3.5 %collective-permute-start.14 = (f32[64,128]{1,0:T(8,128)S(1)}, f32[64,128]{1,0:T(8,128)S(1)}, u32[]{:S(2)}, u32[]{:S(2)}) collective-permute-start(f32[64,128]{1,0:T(8,128)S(1)} %get-tuple-element.51), channel_id=1, source_target_pairs={{0,3},{1,2},{2,1},{3,0},{4,7},{5,6},{6,5},{7,4},{8,11},{9,10},{10,... | collective-permute-start | bytes 98312 | tf_op jit(solution)/shard_map/ppermute | solution.py:367
  59.3 0.0 collective-permute-start.13
  59.3 2.5 %collective-permute-done.14.zo = f32[64,128]{1,0:T(8,128)S(1)} collective-permute-done((f32[64,128]{1,0:T(8,128)S(1)}, f32[64,128]{1,0:T(8,128)S(1)}, u32[]{:S(2)}, u32[]{:S(2)}) %collective-permute-start.14) | collective-permute-done | bytes 32800 | tf_op jit(solution)/shard_map/ppermute | solution.py:367
  61.8 1.4 %collective-permute-done.13.zi = f32[64,128]{1,0:T(8,128)S(1)} collective-permute-done((f32[64,128]{1,0:T(8,128)S(1)}, f32[64,128]{1,0:T(8,128)S(1)}, u32[]{:S(2)}, u32[]{:S(2)}) %collective-permute-start.13) | collective-permute-done | bytes 32800 | tf_op jit(solution)/shard_map/ppermute | solution.py:367
  63.2 0.0 collective-permute-done.12.yi.yo
  63.2 0.0 collective-permute-done.10.xi
  63.2 0.0 collective-permute-done.11.xo
  63.2 14.1 %shard_map.43 = (bf16[8,32,16,128]{3,2,1,0:T(8,128)(2,1)S(1)}, bf16[32,16,128]{2,1,0:T(8,128)(2,1)S(1)}, bf16[32,16,128]{2,1,0:T(8,128)(2,1)S(1)}, f32[128,128]{...) custom-call(s32[12]{0:T(128)S(1)} %stack.66.place, ...), custom_call_target="tpu_custom_call" | custom-call | tf_op jit(solution)/shard_map/pallas_call | solution.py:422
  77.3 0.1 collective-permute-start.15
  77.4 1.3 %collective-permute-done.15.yi.yo = f32[216,128]{1,0:T(8,128)S(1)} collective-permute-done((f32[216,128]{1,0:T(8,128)S(1)}, f32[216,128]{1,0:T(8,128)S(1)}, u32[]{:S(2)}, u32[]{:S(2)}) %collective-permute-start.15) | collective-permute-done | bytes 110624 | tf_op jit(solution)/shard_map/ppermute | solution.py:367
  78.7 1.5 %collective-permute-start.18 = (f32[88,128]{1,0:T(8,128)S(1)}, f32[88,128]{1,0:T(8,128)S(1)}, u32[]{:S(2)}, u32[]{:S(2)}) collective-permute-start(f32[88,128]{1,0:T(8,128)S(1)} %slice_add_fusion.2), channel_id=1, source_target_pairs={{0,16},{8,24},{16,0},{24,8},{1,17},{9,25},{17,1},{25,9},{2,18},{10... | collective-permute-start | bytes 135176 | tf_op jit(solution)/shard_map/ppermute | solution.py:367
  80.2 1.5 %collective-permute-start.17 = (f32[88,128]{1,0:T(8,128)S(1)}, f32[88,128]{1,0:T(8,128)S(1)}, u32[]{:S(2)}, u32[]{:S(2)}) collective-permute-start(f32[88,128]{1,0:T(8,128)S(1)} %slice_add_fusion.2), channel_id=1, source_target_pairs={{0,24},{8,16},{16,8},{24,0},{1,25},{9,17},{17,9},{25,1},{2,26},{10... | collective-permute-start | bytes 135176 | tf_op jit(solution)/shard_map/ppermute | solution.py:367
  81.7 0.5 collective-permute-start.16
  82.3 0.6 collective-permute-done.18
  82.8 2.3 %collective-permute-done.17 = f32[88,128]{1,0:T(8,128)S(1)} collective-permute-done((f32[88,128]{1,0:T(8,128)S(1)}, f32[88,128]{1,0:T(8,128)S(1)}, u32[]{:S(2)}, u32[]{:S(2)}) %collective-permute-start.17) | collective-permute-done | bytes 45088 | tf_op jit(solution)/shard_map/ppermute | solution.py:367
  85.1 0.6 collective-permute-done.16
  85.8 2.5 %collective-permute-start.20 = (f32[152,128]{1,0:T(8,128)S(1)}, f32[152,128]{1,0:T(8,128)S(1)}, u32[]{:S(2)}, u32[]{:S(2)}) collective-permute-start(f32[152,128]{1,0:T(8,128)S(1)} %constant_dynamic-update-slice_fusion.2), channel_id=1, source_target_pairs={{0,3},{1,2},{2,1},{3,0},{4,7},{5,6},{6,5},{7,4},{8,11},{9,10},{10,... | collective-permute-start | bytes 233480 | tf_op jit(solution)/shard_map/ppermute | solution.py:367
  88.3 0.0 collective-permute-start.19
  88.3 2.0 %collective-permute-start.21 = (f32[88,128]{1,0:T(8,128)S(1)}, f32[88,128]{1,0:T(8,128)S(1)}, u32[]{:S(2)}, u32[]{:S(2)}) collective-permute-start(f32[88,128]{1,0:T(8,128)S(1)} %add_add_fusion), channel_id=1, source_target_pairs={{0,2},{1,3},{2,0},{3,1},{4,6},{5,7},{6,4},{7,5},{8,10},{9,11},{10,... | collective-permute-start | bytes 135176 | tf_op jit(solution)/shard_map/ppermute | solution.py:367
  90.2 0.5 collective-permute-start.22
  90.8 1.4 %collective-permute-start.23 = (bf16[32,16,128]{2,1,0:T(8,128)(2,1)S(1)}, bf16[32,16,128]{2,1,0:T(8,128)(2,1)S(1)}, u32[]{:S(2)}, u32[]{:S(2)}) collective-permute-start(bf16[32,16,128]{2,1,0:T(8,128)(2,1)S(1)} %get-tuple-element.59), channel_id=1, source_target_pairs={{0,24},{8,16},{16,8},{24,0},{1,25},{9,17},{17,9},{25,1},{2,26},{10... | collective-permute-start | bytes 393224 | tf_op jit(solution)/shard_map/ppermute | solution.py:367
  92.2 1.2 %collective-permute-done.21 = f32[88,128]{1,0:T(8,128)S(1)} collective-permute-done((f32[88,128]{1,0:T(8,128)S(1)}, f32[88,128]{1,0:T(8,128)S(1)}, u32[]{:S(2)}, u32[]{:S(2)}) %collective-permute-start.21) | collective-permute-done | bytes 45088 | tf_op jit(solution)/shard_map/ppermute | solution.py:367
  93.4 0.0 collective-permute-done.20.zo
  93.4 0.3 collective-permute-done.19.zi
  93.7 1.6 %collective-permute-done.22.xi = bf16[32,16,128]{2,1,0:T(8,128)(2,1)S(1)} collective-permute-done((bf16[32,16,128]{2,1,0:T(8,128)(2,1)S(1)}, bf16[32,16,128]{2,1,0:T(8,128)(2,1)S(1)}, u32[]{:S(2)}, u32[]{:S(2)}) %collective-permute-start.22) | collective-permute-done | bytes 131104 | tf_op jit(solution)/shard_map/ppermute | solution.py:367
  95.3 1.3 %collective-permute-done.23.xo = bf16[32,16,128]{2,1,0:T(8,128)(2,1)S(1)} collective-permute-done((bf16[32,16,128]{2,1,0:T(8,128)(2,1)S(1)}, bf16[32,16,128]{2,1,0:T(8,128)(2,1)S(1)}, u32[]{:S(2)}, u32[]{:S(2)}) %collective-permute-start.23) | collective-permute-done | bytes 131104 | tf_op jit(solution)/shard_map/ppermute | solution.py:367
  96.7 0.0 collective-permute-start.24
  96.7 1.2 %collective-permute-done.24.theirs = f32[88,128]{1,0:T(8,128)S(1)} collective-permute-done((f32[88,128]{1,0:T(8,128)S(1)}, f32[88,128]{1,0:T(8,128)S(1)}, u32[]{:S(2)}, u32[]{:S(2)}) %collective-permute-start.24) | collective-permute-done | bytes 45088 | tf_op jit(solution)/shard_map/ppermute | solution.py:367
  97.9 13.5 %shard_map.44 = (bf16[16,8,32,128]{3,2,1,0:T(8,128)(2,1)}, f32[16,32]{1,0:T(8,128)}) custom-call(s32[12]{0:T(128)S(1)} %stack.66.place, f32[88,128]{1,0:T(8,128)S(1)} %fusion.mine, f32[88,128]{1,0:T(8,128)S(1)} %collective-permute-done.24.theirs, bf16[8,32,32,128]{3,2,1,0:T(8,128)(2,1)S(1)} %get-tuple-element.42.xt, ...), custom_call_target="tpu_custom_call" | custom-call | tf_op jit(solution)/shard_map/pallas_call | solution.py:422
  (10 shorter events, 0.1 us)
Async XLA Ops:
  0.8 1.2 %copy-start = (bf16[16,8,32,128]{3,2,1,0:T(8,128)(2,1)S(1)}, bf16[16,8,32,128]{3,2,1,0:T(8,128)(2,1)}, u32[]{:S(2)}) copy-start(bf16[16,8,32,128]{3,2,1,0:T(8,128)(2,1)} %q_hbm.1) | copy-start | bytes 3145732
  15.7 1.5 %collective-permute-start = (f32[216,128]{1,0:T(8,128)S(1)}, f32[216,128]{1,0:T(8,128)S(1)}, u32[]{:S(2)}, u32[]{:S(2)}) collective-permute-start(f32[216,128]{1,0:T(8,128)S(1)} %get-tuple-element.34), channel_id=1, source_target_pairs={{0,4},{4,0},{1,5},{5,1},{2,6},{6,2},{3,7},{7,3},{8,12},{12,8},{9,1... | collective-permute-start | bytes 331784 | tf_op jit(solution)/shard_map/ppermute | solution.py:367
  17.2 5.0 %collective-permute-start.3 = (f32[88,128]{1,0:T(8,128)S(1)}, f32[88,128]{1,0:T(8,128)S(1)}, u32[]{:S(2)}, u32[]{:S(2)}) collective-permute-start(f32[88,128]{1,0:T(8,128)S(1)} %slice_add_fusion.5), channel_id=1, source_target_pairs={{0,16},{8,24},{16,0},{24,8},{1,17},{9,25},{17,1},{25,9},{2,18},{10... | collective-permute-start | bytes 135176 | tf_op jit(solution)/shard_map/ppermute | solution.py:367
  20.1 5.4 %collective-permute-start.2 = (f32[88,128]{1,0:T(8,128)S(1)}, f32[88,128]{1,0:T(8,128)S(1)}, u32[]{:S(2)}, u32[]{:S(2)}) collective-permute-start(f32[88,128]{1,0:T(8,128)S(1)} %slice_add_fusion.5), channel_id=1, source_target_pairs={{0,24},{8,16},{16,8},{24,0},{1,25},{9,17},{17,9},{25,1},{2,26},{10... | collective-permute-start | bytes 135176 | tf_op jit(solution)/shard_map/ppermute | solution.py:367
  21.5 4.0 %collective-permute-start.1 = (f32[88,128]{1,0:T(8,128)S(1)}, f32[88,128]{1,0:T(8,128)S(1)}, u32[]{:S(2)}, u32[]{:S(2)}) collective-permute-start(f32[88,128]{1,0:T(8,128)S(1)} %slice_add_fusion.5), channel_id=1, source_target_pairs={{0,8},{8,0},{16,24},{24,16},{1,9},{9,1},{17,25},{25,17},{2,10},{10... | collective-permute-start | bytes 135176 | tf_op jit(solution)/shard_map/ppermute | solution.py:367
  25.6 8.6 %collective-permute-start.5 = (f32[152,128]{1,0:T(8,128)S(1)}, f32[152,128]{1,0:T(8,128)S(1)}, u32[]{:S(2)}, u32[]{:S(2)}) collective-permute-start(f32[152,128]{1,0:T(8,128)S(1)} %constant_dynamic-update-slice_fusion), channel_id=1, source_target_pairs={{0,3},{1,2},{2,1},{3,0},{4,7},{5,6},{6,5},{7,4},{8,11},{9,10},{10,... | collective-permute-start | bytes 233480 | tf_op jit(solution)/shard_map/ppermute | solution.py:367
  29.3 5.0 %collective-permute-start.4 = (f32[152,128]{1,0:T(8,128)S(1)}, f32[152,128]{1,0:T(8,128)S(1)}, u32[]{:S(2)}, u32[]{:S(2)}) collective-permute-start(f32[152,128]{1,0:T(8,128)S(1)} %constant_dynamic-update-slice_fusion), channel_id=1, source_target_pairs={{0,1},{1,0},{2,3},{3,2},{4,5},{5,4},{6,7},{7,6},{8,9},{9,8},{10,11... | collective-permute-start | bytes 233480 | tf_op jit(solution)/shard_map/ppermute | solution.py:367
  29.3 4.9 %collective-permute-start.6 = (f32[88,128]{1,0:T(8,128)S(1)}, f32[88,128]{1,0:T(8,128)S(1)}, u32[]{:S(2)}, u32[]{:S(2)}) collective-permute-start(f32[88,128]{1,0:T(8,128)S(1)} %add_add_fusion.1), channel_id=1, source_target_pairs={{0,2},{1,3},{2,0},{3,1},{4,6},{5,7},{6,4},{7,5},{8,10},{9,11},{10,... | collective-permute-start | bytes 135176 | tf_op jit(solution)/shard_map/ppermute | solution.py:367
  30.1 5.2 %collective-permute-start.7 = (bf16[32,16,128]{2,1,0:T(8,128)(2,1)S(1)}, bf16[32,16,128]{2,1,0:T(8,128)(2,1)S(1)}, u32[]{:S(2)}, u32[]{:S(2)}) collective-permute-start(bf16[32,16,128]{2,1,0:T(8,128)(2,1)S(1)} %get-tuple-element.39), channel_id=1, source_target_pairs={{0,8},{8,0},{16,24},{24,16},{1,9},{9,1},{17,25},{25,17},{2,10},{10... | collective-permute-start | bytes 393224 | tf_op jit(solution)/shard_map/ppermute | solution.py:367
  31.0 6.5 %collective-permute-start.8 = (bf16[32,16,128]{2,1,0:T(8,128)(2,1)S(1)}, bf16[32,16,128]{2,1,0:T(8,128)(2,1)S(1)}, u32[]{:S(2)}, u32[]{:S(2)}) collective-permute-start(bf16[32,16,128]{2,1,0:T(8,128)(2,1)S(1)} %get-tuple-element.40), channel_id=1, source_target_pairs={{0,24},{8,16},{16,8},{24,0},{1,25},{9,17},{17,9},{25,1},{2,26},{10... | collective-permute-start | bytes 393224 | tf_op jit(solution)/shard_map/ppermute | solution.py:367
  37.5 1.2 %collective-permute-start.9 = (f32[88,128]{1,0:T(8,128)S(1)}, f32[88,128]{1,0:T(8,128)S(1)}, u32[]{:S(2)}, u32[]{:S(2)}) collective-permute-start(f32[88,128]{1,0:T(8,128)S(1)} %fusion.1.mine), channel_id=1, source_target_pairs={{0,4},{4,0},{1,5},{5,1},{2,6},{6,2},{3,7},{7,3},{8,12},{12,8},{9,1... | collective-permute-start | bytes 135176 | tf_op jit(solution)/shard_map/ppermute | solution.py:367
  53.7 9.5 %collective-permute-start.10 = (bf16[32,16,128]{2,1,0:T(8,128)(2,1)S(1)}, bf16[32,16,128]{2,1,0:T(8,128)(2,1)S(1)}, u32[]{:S(2)}, u32[]{:S(2)}) collective-permute-start(bf16[32,16,128]{2,1,0:T(8,128)(2,1)S(1)} %get-tuple-element.48), channel_id=1, source_target_pairs={{0,8},{8,0},{16,24},{24,16},{1,9},{9,1},{17,25},{25,17},{2,10},{10... | collective-permute-start | bytes 393224 | tf_op jit(solution)/shard_map/ppermute | solution.py:367
  54.2 9.0 %collective-permute-start.11 = (bf16[32,16,128]{2,1,0:T(8,128)(2,1)S(1)}, bf16[32,16,128]{2,1,0:T(8,128)(2,1)S(1)}, u32[]{:S(2)}, u32[]{:S(2)}) collective-permute-start(bf16[32,16,128]{2,1,0:T(8,128)(2,1)S(1)} %get-tuple-element.49), channel_id=1, source_target_pairs={{0,24},{8,16},{16,8},{24,0},{1,25},{9,17},{17,9},{25,1},{2,26},{10... | collective-permute-start | bytes 393224 | tf_op jit(solution)/shard_map/ppermute | solution.py:367
  55.8 7.4 %collective-permute-start.12 = (f32[128,128]{1,0:T(8,128)S(1)}, f32[128,128]{1,0:T(8,128)S(1)}, u32[]{:S(2)}, u32[]{:S(2)}) collective-permute-start(f32[128,128]{1,0:T(8,128)S(1)} %get-tuple-element.50), channel_id=1, source_target_pairs={{0,4},{4,0},{1,5},{5,1},{2,6},{6,2},{3,7},{7,3},{8,12},{12,8},{9,1... | collective-permute-start | bytes 196616 | tf_op jit(solution)/shard_map/ppermute | solution.py:367
  55.8 6.0 %collective-permute-start.14 = (f32[64,128]{1,0:T(8,128)S(1)}, f32[64,128]{1,0:T(8,128)S(1)}, u32[]{:S(2)}, u32[]{:S(2)}) collective-permute-start(f32[64,128]{1,0:T(8,128)S(1)} %get-tuple-element.51), channel_id=1, source_target_pairs={{0,3},{1,2},{2,1},{3,0},{4,7},{5,6},{6,5},{7,4},{8,11},{9,10},{10,... | collective-permute-start | bytes 98312 | tf_op jit(solution)/shard_map/ppermute | solution.py:367
  59.3 3.9 %collective-permute-start.13 = (f32[64,128]{1,0:T(8,128)S(1)}, f32[64,128]{1,0:T(8,128)S(1)}, u32[]{:S(2)}, u32[]{:S(2)}) collective-permute-start(f32[64,128]{1,0:T(8,128)S(1)} %get-tuple-element.51), channel_id=1, source_target_pairs={{0,1},{1,0},{2,3},{3,2},{4,5},{5,4},{6,7},{7,6},{8,9},{9,8},{10,11... | collective-permute-start | bytes 98312 | tf_op jit(solution)/shard_map/ppermute | solution.py:367
  77.3 1.4 %collective-permute-start.15 = (f32[216,128]{1,0:T(8,128)S(1)}, f32[216,128]{1,0:T(8,128)S(1)}, u32[]{:S(2)}, u32[]{:S(2)}) collective-permute-start(f32[216,128]{1,0:T(8,128)S(1)} %get-tuple-element.53), channel_id=1, source_target_pairs={{0,4},{4,0},{1,5},{5,1},{2,6},{6,2},{3,7},{7,3},{8,12},{12,8},{9,1... | collective-permute-start | bytes 331784 | tf_op jit(solution)/shard_map/ppermute | solution.py:367
  78.7 4.1 %collective-permute-start.18 = (f32[88,128]{1,0:T(8,128)S(1)}, f32[88,128]{1,0:T(8,128)S(1)}, u32[]{:S(2)}, u32[]{:S(2)}) collective-permute-start(f32[88,128]{1,0:T(8,128)S(1)} %slice_add_fusion.2), channel_id=1, source_target_pairs={{0,16},{8,24},{16,0},{24,8},{1,17},{9,25},{17,1},{25,9},{2,18},{10... | collective-permute-start | bytes 135176 | tf_op jit(solution)/shard_map/ppermute | solution.py:367
  80.2 4.9 %collective-permute-start.17 = (f32[88,128]{1,0:T(8,128)S(1)}, f32[88,128]{1,0:T(8,128)S(1)}, u32[]{:S(2)}, u32[]{:S(2)}) collective-permute-start(f32[88,128]{1,0:T(8,128)S(1)} %slice_add_fusion.2), channel_id=1, source_target_pairs={{0,24},{8,16},{16,8},{24,0},{1,25},{9,17},{17,9},{25,1},{2,26},{10... | collective-permute-start | bytes 135176 | tf_op jit(solution)/shard_map/ppermute | solution.py:367
  81.7 4.0 %collective-permute-start.16 = (f32[88,128]{1,0:T(8,128)S(1)}, f32[88,128]{1,0:T(8,128)S(1)}, u32[]{:S(2)}, u32[]{:S(2)}) collective-permute-start(f32[88,128]{1,0:T(8,128)S(1)} %slice_add_fusion.2), channel_id=1, source_target_pairs={{0,8},{8,0},{16,24},{24,16},{1,9},{9,1},{17,25},{25,17},{2,10},{10... | collective-permute-start | bytes 135176 | tf_op jit(solution)/shard_map/ppermute | solution.py:367
  85.8 7.6 %collective-permute-start.20 = (f32[152,128]{1,0:T(8,128)S(1)}, f32[152,128]{1,0:T(8,128)S(1)}, u32[]{:S(2)}, u32[]{:S(2)}) collective-permute-start(f32[152,128]{1,0:T(8,128)S(1)} %constant_dynamic-update-slice_fusion.2), channel_id=1, source_target_pairs={{0,3},{1,2},{2,1},{3,0},{4,7},{5,6},{6,5},{7,4},{8,11},{9,10},{10,... | collective-permute-start | bytes 233480 | tf_op jit(solution)/shard_map/ppermute | solution.py:367
  88.3 5.4 %collective-permute-start.19 = (f32[152,128]{1,0:T(8,128)S(1)}, f32[152,128]{1,0:T(8,128)S(1)}, u32[]{:S(2)}, u32[]{:S(2)}) collective-permute-start(f32[152,128]{1,0:T(8,128)S(1)} %constant_dynamic-update-slice_fusion.2), channel_id=1, source_target_pairs={{0,1},{1,0},{2,3},{3,2},{4,5},{5,4},{6,7},{7,6},{8,9},{9,8},{10,11... | collective-permute-start | bytes 233480 | tf_op jit(solution)/shard_map/ppermute | solution.py:367
  88.3 5.1 %collective-permute-start.21 = (f32[88,128]{1,0:T(8,128)S(1)}, f32[88,128]{1,0:T(8,128)S(1)}, u32[]{:S(2)}, u32[]{:S(2)}) collective-permute-start(f32[88,128]{1,0:T(8,128)S(1)} %add_add_fusion), channel_id=1, source_target_pairs={{0,2},{1,3},{2,0},{3,1},{4,6},{5,7},{6,4},{7,5},{8,10},{9,11},{10,... | collective-permute-start | bytes 135176 | tf_op jit(solution)/shard_map/ppermute | solution.py:367
  90.2 5.1 %collective-permute-start.22 = (bf16[32,16,128]{2,1,0:T(8,128)(2,1)S(1)}, bf16[32,16,128]{2,1,0:T(8,128)(2,1)S(1)}, u32[]{:S(2)}, u32[]{:S(2)}) collective-permute-start(bf16[32,16,128]{2,1,0:T(8,128)(2,1)S(1)} %get-tuple-element.58), channel_id=1, source_target_pairs={{0,8},{8,0},{16,24},{24,16},{1,9},{9,1},{17,25},{25,17},{2,10},{10... | collective-permute-start | bytes 393224 | tf_op jit(solution)/shard_map/ppermute | solution.py:367
  90.8 5.9 %collective-permute-start.23 = (bf16[32,16,128]{2,1,0:T(8,128)(2,1)S(1)}, bf16[32,16,128]{2,1,0:T(8,128)(2,1)S(1)}, u32[]{:S(2)}, u32[]{:S(2)}) collective-permute-start(bf16[32,16,128]{2,1,0:T(8,128)(2,1)S(1)} %get-tuple-element.59), channel_id=1, source_target_pairs={{0,24},{8,16},{16,8},{24,0},{1,25},{9,17},{17,9},{25,1},{2,26},{10... | collective-permute-start | bytes 393224 | tf_op jit(solution)/shard_map/ppermute | solution.py:367
  96.7 1.2 %collective-permute-start.24 = (f32[88,128]{1,0:T(8,128)S(1)}, f32[88,128]{1,0:T(8,128)S(1)}, u32[]{:S(2)}, u32[]{:S(2)}) collective-permute-start(f32[88,128]{1,0:T(8,128)S(1)} %fusion.mine), channel_id=1, source_target_pairs={{0,4},{4,0},{1,5},{5,1},{2,6},{6,2},{3,7},{7,3},{8,12},{12,8},{9,1... | collective-permute-start | bytes 135176 | tf_op jit(solution)/shard_map/ppermute | solution.py:367
